TPU v7x, 32 devices: a whole 2x2x4 slice. The times are simulated.
32 devices in a mesh: section: 2 (over y), tensor: 4 (over z), dp: 4 (over x, core).
Axes of the slice: x: 2, y: 2, z: 4, core: 2. Of those that a mesh axis runs over, the one named last changes fastest.
Arguments:
- block_input: bfloat16 [8, 1024, 1024], P('dp', 'tensor'), may hold values from -6 to 6
- cotangent: bfloat16 [8, 1024, 1024], P('dp', 'tensor'), may hold values from -6 to 6
- first_gain: bfloat16 [2, 1024], P('section'), may hold values from 0.25 to 1.75
- first_shift: bfloat16 [2, 1024], P('section'), may hold values from -1.25 to 1.25
- attend_weight: bfloat16 [2, 1024, 3, 1024], P('section', None, None, 'tensor'), may hold values from -0.1875 to 0.1875
- attend_bias: bfloat16 [2, 2, 1024], P('section', None, 'tensor'), may hold values from -3 to 3
- mixing_weight: bfloat16 [2, 1024, 1024], P('section', 'tensor'), may hold values from -1.5 to 1.5
- mixing_bias: bfloat16 [2, 1024], P('section'), may hold values from -1.25 to 1.25
- second_gain: bfloat16 [2, 1024], P('section'), may hold values from 0.25 to 1.75
- second_shift: bfloat16 [2, 1024], P('section'), may hold values from -1.25 to 1.25
- expand_weight: bfloat16 [2, 1024, 4096], P('section', None, 'tensor'), may hold values from -0.1875 to 0.1875
- expand_bias: bfloat16 [2, 4096], P('section', 'tensor'), may hold values from -1.25 to 1.25
- shrink_weight: bfloat16 [2, 1024, 4096], P('section', None, 'tensor'), may hold values from -0.09375 to 0.09375
- shrink_bias: bfloat16 [2, 1024], P('section'), may hold values from -1.25 to 1.25
Outputs:
- section_output: bfloat16 [2, 8, 1024, 1024], P('section', 'dp', 'tensor')
- input_change: bfloat16 [2, 8, 1024, 1024], P('section', 'dp', 'tensor')
- first_gain_gradient: float32 [2, 1024], P('section')
- first_shift_gradient: float32 [2, 1024], P('section')
- attend_weight_gradient: float32 [2, 1024, 3, 1024], P('section', None, None, 'tensor')
- attend_bias_gradient: float32 [2, 2, 1024], P('section', None, 'tensor')
- mixing_weight_gradient: float32 [2, 1024, 1024], P('section', 'tensor')
- mixing_bias_gradient: float32 [2, 1024], P('section')
- second_gain_gradient: float32 [2, 1024], P('section')
- second_shift_gradient: float32 [2, 1024], P('section')
- expand_weight_gradient: float32 [2, 1024, 4096], P('section', None, 'tensor')
- expand_bias_gradient: float32 [2, 4096], P('section', 'tensor')
- shrink_weight_gradient: float32 [2, 1024, 4096], P('section', None, 'tensor')
- shrink_bias_gradient: float32 [2, 1024], P('section')
All inputs are finite; a program needn't handle non-finite values.
Results may differ from a plain program's by a relative error of at most 0.017.
Values may be sent and summed in bfloat16 or wider, within the bound.
A program may use at most 192 MiB of HBM per device.

v0:
```python
import jax
import jax.numpy as jnp
from jax import lax
from jax.sharding import PartitionSpec as P

HD = 64


epsilon = 1e-05
contract_rows = (((0,), (0,)), ((), ()))
contract_last = (((1,), (1,)), ((), ()))


def from_behind(block, axis, distance):
    devices = range(lax.axis_size(axis))
    route = [(i - distance, i) for i in devices if i - distance in devices]
    return lax.ppermute(block, axis, route)


def layer_norm(values, gain_row, shift_row):
    center = values - jnp.mean(values, axis=-1, keepdims=True)
    spread = jnp.mean(center * center, axis=-1, keepdims=True)
    return center * lax.rsqrt(spread + epsilon) * gain_row + shift_row


def smooth_gate(values):
    return jax.nn.gelu(values, approximate=True)


def causal_scores(query_block, key_rows, row_first, scaling):
    block_rows = query_block.shape[0]
    length = key_rows.shape[0]
    scores = (
        jnp.einsum("qhd,khd->hqk", query_block, key_rows, preferred_element_type=jnp.float32)
        * scaling
    )
    row_ids = row_first + lax.broadcasted_iota(jnp.int32, (block_rows, length), 0)
    col_ids = lax.broadcasted_iota(jnp.int32, (block_rows, length), 1)
    return jnp.where((row_ids >= col_ids)[None], scores, -jnp.inf)


def attend_forward(queries, key_rows, value_rows, scaling):
    length = queries.shape[0]
    block_rows = min(512, length)
    firsts = jnp.arange(length // block_rows, dtype=jnp.int32) * block_rows

    def one_block(row_first):
        query_block = lax.dynamic_slice_in_dim(queries, row_first, block_rows, 0)
        scores = causal_scores(query_block, key_rows, row_first, scaling)
        largest = jnp.max(scores, axis=-1, keepdims=True)
        weights = jnp.exp(scores - largest)
        totals = jnp.sum(weights, axis=-1, keepdims=True)
        shares = (weights / totals).astype(jnp.bfloat16)
        blended = jnp.einsum("hqk,khd->qhd", shares, value_rows, preferred_element_type=jnp.float32)
        return (blended, (largest + jnp.log(totals))[..., 0])

    blended, logsum = lax.map(one_block, firsts)
    return (blended.reshape(length, -1), logsum)


def attend_backward(queries, key_rows, value_rows, blended_change, logsum, scaling):
    length = queries.shape[0]
    block_rows = logsum.shape[2]
    firsts = jnp.arange(length // block_rows, dtype=jnp.int32) * block_rows

    def one_block(running, inputs):
        key_change, value_change = running
        row_first, block_logsum = inputs
        query_block = lax.dynamic_slice_in_dim(queries, row_first, block_rows, 0)
        change_block = lax.dynamic_slice_in_dim(blended_change, row_first, block_rows, 0)
        scores = causal_scores(query_block, key_rows, row_first, scaling)
        shares = jnp.exp(scores - block_logsum[..., None])
        share_change = jnp.einsum(
            "qhd,khd->hqk", change_block, value_rows, preferred_element_type=jnp.float32
        )
        row_inner = jnp.sum(share_change * shares, axis=-1, keepdims=True)
        score_change = (shares * (share_change - row_inner)).astype(jnp.bfloat16)
        query_change = (
            jnp.einsum("hqk,khd->qhd", score_change, key_rows, preferred_element_type=jnp.float32)
            * scaling
        )
        key_change = (
            key_change
            + jnp.einsum(
                "hqk,qhd->khd", score_change, query_block, preferred_element_type=jnp.float32
            )
            * scaling
        )
        value_change = value_change + jnp.einsum(
            "hqk,qhd->khd",
            shares.astype(jnp.bfloat16),
            change_block,
            preferred_element_type=jnp.float32,
        )
        return ((key_change, value_change), query_change)

    start_zeros = jnp.zeros(key_rows.shape, jnp.float32)
    (key_change, value_change), query_change = lax.scan(
        one_block, (start_zeros, start_zeros), (firsts, logsum)
    )
    return (query_change.reshape(queries.shape), key_change, value_change)


def body(
    block_input,
    cotangent,
    first_gain,
    first_shift,
    attend_weight,
    attend_bias,
    mixing_weight,
    mixing_bias,
    second_gain,
    second_shift,
    expand_weight,
    expand_bias,
    shrink_weight,
    shrink_bias,
):
    micro_count, local_rows, model_width = block_input.shape
    local_width = attend_weight.shape[3]
    local_heads = local_width // HD
    scaling = HD ** (-0.5)
    section_index = lax.axis_index("section")
    gain_one = first_gain[0].astype(jnp.float32)
    shift_one = first_shift[0].astype(jnp.float32)
    gain_two = second_gain[0].astype(jnp.float32)
    shift_two = second_shift[0].astype(jnp.float32)
    mixing_offset = mixing_bias[0].astype(jnp.float32)
    shrink_offset = shrink_bias[0].astype(jnp.float32)
    attend_matrix = attend_weight[0].reshape(model_width, 3 * local_width)
    bias_pair = attend_bias[0].astype(jnp.float32)
    attend_offset = jnp.concatenate([bias_pair[0], jnp.zeros_like(bias_pair[0]), bias_pair[1]])
    mixing_matrix = mixing_weight[0]
    expand_matrix = expand_weight[0]
    shrink_matrix = shrink_weight[0]
    expand_offset = expand_bias.astype(jnp.float32)

    def forward_tick(received, step_index):
        own_input = lax.dynamic_index_in_dim(
            block_input, jnp.minimum(step_index, micro_count - 1), 0, keepdims=False
        )
        layer_input = jnp.where(section_index == 0, own_input, received)
        residual = layer_input.astype(jnp.float32)
        normed = layer_norm(residual, gain_one, shift_one).astype(jnp.bfloat16)
        normed_full = lax.all_gather(normed, "tensor", axis=0, tiled=True)
        length = normed_full.shape[0]
        projected = (
            jnp.dot(normed_full, attend_matrix, preferred_element_type=jnp.float32) + attend_offset
        ).astype(jnp.bfloat16)
        head_split = projected.reshape(length, 3, local_heads, HD)
        blended, logsum = attend_forward(
            head_split[:, 0], head_split[:, 1], head_split[:, 2], scaling
        )
        blended = blended.astype(jnp.bfloat16)
        middle = (
            residual
            + lax.psum_scatter(
                jnp.dot(blended, mixing_matrix, preferred_element_type=jnp.float32),
                "tensor",
                scatter_dimension=0,
                tiled=True,
            )
            + mixing_offset
        )
        second = layer_norm(middle, gain_two, shift_two).astype(jnp.bfloat16)
        feed_input = lax.all_gather(second, "tensor", axis=0, tiled=True)
        hidden_pre = (
            jnp.dot(feed_input, expand_matrix, preferred_element_type=jnp.float32) + expand_offset
        )
        hidden = smooth_gate(hidden_pre).astype(jnp.bfloat16)
        branch = lax.psum_scatter(
            lax.dot_general(
                hidden, shrink_matrix, contract_last, preferred_element_type=jnp.float32
            ).astype(jnp.bfloat16),
            "tensor",
            scatter_dimension=0,
            tiled=True,
        ).astype(jnp.float32)
        result = (middle + branch + shrink_offset).astype(jnp.bfloat16)
        passed = from_behind(result, "section", 1)
        return (
            passed,
            (
                layer_input,
                normed_full,
                projected,
                logsum,
                blended,
                middle,
                feed_input,
                hidden_pre,
                result,
            ),
        )

    first_carry = jnp.zeros((local_rows, model_width), jnp.bfloat16)
    tick_steps = jnp.arange(micro_count + 1, dtype=jnp.int32)
    final_forward, kept_ticks = lax.scan(forward_tick, first_carry, tick_steps)
    kept = jax.tree.map(
        lambda stacked: lax.dynamic_slice_in_dim(stacked, section_index, micro_count, 0), kept_ticks
    )
    section_output = kept[8][None]

    def backward_tick(running, step_index):
        received, running_sums = running
        micro_index = step_index - 1 + section_index
        in_range = (micro_index >= 0) & (micro_index < micro_count)
        clamped = jnp.clip(micro_index, 0, micro_count - 1)
        (
            layer_input,
            normed_full,
            projected,
            logsum,
            blended,
            middle,
            feed_input,
            hidden_pre,
            result,
        ) = jax.tree.map(
            lambda stacked: lax.dynamic_index_in_dim(stacked, clamped, 0, keepdims=False), kept
        )
        given_change = lax.dynamic_index_in_dim(cotangent, clamped, 0, keepdims=False)
        given_change = jnp.where(in_range, given_change, jnp.zeros_like(given_change))
        out_change = jnp.where(section_index == 1, given_change, received)
        gate_value, gate_back = jax.vjp(smooth_gate, hidden_pre)
        hidden = gate_value.astype(jnp.bfloat16)
        change_full = lax.all_gather(out_change, "tensor", axis=0, tiled=True)
        shrink_change = lax.dot_general(
            change_full, hidden, contract_rows, preferred_element_type=jnp.float32
        )
        pre_change = gate_back(
            jnp.dot(change_full, shrink_matrix, preferred_element_type=jnp.float32)
        )[0].astype(jnp.bfloat16)
        expand_change = lax.dot_general(
            feed_input, pre_change, contract_rows, preferred_element_type=jnp.float32
        )
        expand_row_change = jnp.sum(pre_change.astype(jnp.float32), axis=0, keepdims=True)
        second_change = lax.psum_scatter(
            lax.dot_general(
                pre_change, expand_matrix, contract_last, preferred_element_type=jnp.float32
            ).astype(jnp.bfloat16),
            "tensor",
            scatter_dimension=0,
            tiled=True,
        ).astype(jnp.float32)
        middle_norm, gain_two_change, shift_two_change = jax.vjp(
            layer_norm, middle, gain_two, shift_two
        )[1](second_change)
        out_float = out_change.astype(jnp.float32)
        middle_change = out_float + middle_norm
        branch_full = lax.all_gather(
            middle_change.astype(jnp.bfloat16), "tensor", axis=0, tiled=True
        )
        mixing_change = lax.dot_general(
            blended, branch_full, contract_rows, preferred_element_type=jnp.float32
        )
        blended_change = lax.dot_general(
            branch_full, mixing_matrix, contract_last, preferred_element_type=jnp.float32
        ).astype(jnp.bfloat16)
        length = branch_full.shape[0]
        head_split = projected.reshape(length, 3, local_heads, HD)
        query_change, key_change, value_change = attend_backward(
            head_split[:, 0],
            head_split[:, 1],
            head_split[:, 2],
            blended_change.reshape(length, local_heads, HD),
            logsum,
            scaling,
        )
        projected_change = (
            jnp.stack([query_change, key_change, value_change], axis=1)
            .reshape(length, 3 * local_width)
            .astype(jnp.bfloat16)
        )
        attend_change = lax.dot_general(
            normed_full, projected_change, contract_rows, preferred_element_type=jnp.float32
        )
        column_sums = jnp.sum(projected_change.astype(jnp.float32), axis=0).reshape(3, local_width)
        bias_change = jnp.stack([column_sums[0], column_sums[2]])
        first_change = lax.psum_scatter(
            lax.dot_general(
                projected_change, attend_matrix, contract_last, preferred_element_type=jnp.float32
            ).astype(jnp.bfloat16),
            "tensor",
            scatter_dimension=0,
            tiled=True,
        ).astype(jnp.float32)
        input_norm, gain_one_change, shift_one_change = jax.vjp(
            layer_norm, layer_input.astype(jnp.float32), gain_one, shift_one
        )[1](first_change)
        input_change = (middle_change + input_norm).astype(jnp.bfloat16)
        passed = from_behind(input_change, "section", -1)
        additions = (
            attend_change,
            bias_change,
            mixing_change,
            expand_change,
            expand_row_change,
            shrink_change,
            gain_one_change,
            shift_one_change,
            jnp.sum(middle_change, axis=0),
            gain_two_change,
            shift_two_change,
            jnp.sum(out_float, axis=0),
        )
        running_sums = tuple(
            (running_sum + addition for running_sum, addition in zip(running_sums, additions))
        )
        return ((passed, running_sums), input_change)

    expand_columns = expand_matrix.shape[1]
    zero_sums = (
        jnp.zeros((model_width, 3 * local_width), jnp.float32),
        jnp.zeros((2, local_width), jnp.float32),
        jnp.zeros((local_width, model_width), jnp.float32),
        jnp.zeros((model_width, expand_columns), jnp.float32),
        jnp.zeros((1, expand_columns), jnp.float32),
        jnp.zeros((model_width, expand_columns), jnp.float32),
    )
    zero_sums = zero_sums + tuple((jnp.zeros((model_width,), jnp.float32) for repeat in range(6)))
    (final_backward, sums), input_ticks = lax.scan(
        backward_tick, (first_carry, zero_sums), tick_steps
    )
    input_changes = lax.dynamic_slice_in_dim(input_ticks, 1 - section_index, micro_count, 0)[None]
    attend_total, bias_total, mixing_total, expand_total, expand_row_total, shrink_total = sums[:6]
    attend_total, bias_total, mixing_total, expand_total, expand_row_total, shrink_total = (
        lax.psum(attend_total.astype(jnp.bfloat16), "dp").astype(jnp.float32),
        lax.psum(bias_total.astype(jnp.bfloat16), "dp").astype(jnp.float32),
        lax.psum(mixing_total.astype(jnp.bfloat16), "dp").astype(jnp.float32),
        lax.psum(expand_total.astype(jnp.bfloat16), "dp").astype(jnp.float32),
        lax.psum(expand_row_total.astype(jnp.bfloat16), "dp").astype(jnp.float32),
        lax.psum(shrink_total.astype(jnp.bfloat16), "dp").astype(jnp.float32),
    )
    (
        gain_one_total,
        shift_one_total,
        mixing_bias_total,
        gain_two_total,
        shift_two_total,
        shrink_bias_total,
    ) = lax.psum((sums[6], sums[7], sums[8], sums[9], sums[10], sums[11]), ("tensor", "dp"))
    return (
        section_output,
        input_changes,
        gain_one_total[None],
        shift_one_total[None],
        attend_total.reshape(1, model_width, 3, local_width),
        bias_total[None],
        mixing_total[None],
        mixing_bias_total[None],
        gain_two_total[None],
        shift_two_total[None],
        expand_total[None],
        expand_row_total,
        shrink_total[None],
        shrink_bias_total[None],
    )


def solution(mesh):
    placed = (
        P("dp", "tensor", None),
        P("dp", "tensor", None),
        P("section", None),
        P("section", None),
        P("section", None, None, "tensor"),
        P("section", None, "tensor"),
        P("section", "tensor", None),
        P("section", None),
        P("section", None),
        P("section", None),
        P("section", None, "tensor"),
        P("section", "tensor"),
        P("section", None, "tensor"),
        P("section", None),
    )
    return jax.shard_map(
        body,
        mesh=mesh,
        in_specs=placed,
        out_specs=(
            P("section", "dp", "tensor", None),
            P("section", "dp", "tensor", None),
            P("section", None),
            P("section", None),
            P("section", None, None, "tensor"),
            P("section", None, "tensor"),
            P("section", "tensor", None),
            P("section", None),
            P("section", None),
            P("section", None),
            P("section", None, "tensor"),
            P("section", "tensor"),
            P("section", None, "tensor"),
            P("section", None),
        ),
        check_vma=False,
    )
```

profile of v0, /device:TPU:0, one launch (start us, length us, event | category | flops | bytes accessed | tf_op | source)
XLA Modules:
  0.0 1934.0 jit_solution(10663872744819147794)
XLA Ops:
  15.9 838.4 %while.121 = (s32[]{:T(128)}, bf16[256,1024]{1,0:T(8,128)(2,1)S(1)}, bf16[3,256,1024]{2,1,0:T(8,128)(2,1)}, bf16[3,1024,1024]{2,1,0:T(8,128)(2,1)}, bf16[3,1024,...) while((s32[]{:T(128)}, bf16[256,1024]{1,0:T(8,128)(2,1)S(1)}, ...), condition=%wide.region_11.12_spmd, body=%wide.region_0.11_spmd.sunk | while | flops 7026768896 | bytes 151415232 | solution.py:199
  20.9 48.7 %all-gather.5.cloned.1.call-done = bf16[1024,1024]{1,0:T(8,128)(2,1)} async-done(((bf16[256,1024]{1,0:T(8,128)(2,1)}), bf16[1024,1024]{1,0:T(8,128)(2,1)}) %all-gather.5.cloned.1.call-update) | async-done | bytes 2097168 | tf_op jit(solution)/shard_map/while/body/eval_jaxpr/all_gather | solution.py:146
  75.2 22.0 %while.124 = (s32[]{:T(128)}, bf16[2,512,4,64]{1,3,2,0:T(8,128)(2,1)S(1)}, f32[2,4,512]{2,1,0:T(4,128)S(1)}, s32[2]{0:T(128)S(1)}, bf16[1024,4,64]{0,2,1:T(8,128...) while((s32[]{:T(128)}, ...), condition=%wide.region_6.6_spmd, body=%wide.region_3.5_spmd.sunk | while | flops 562559488 | bytes 31264968 | solution.py:57
  100.6 75.6 %reduce-scatter.5.cloned.1.call-done = f32[256,1024]{1,0:T(8,128)} async-done(((f32[1024,1024]{1,0:T(8,128)}), f32[256,1024]{1,0:T(8,128)}) %reduce-scatter.5.cloned.1.call-update) | async-done | bytes 1048592 | tf_op jit(solution)/shard_map/while/body/eval_jaxpr/reduce_scatter | solution.py:158
  180.2 46.5 %all-gather.7.cloned.1.call-done = bf16[1024,1024]{1,0:T(8,128)(2,1)} async-done(((bf16[256,1024]{1,0:T(8,128)(2,1)}), bf16[1024,1024]{1,0:T(8,128)(2,1)}) %all-gather.7.cloned.1.call-update) | async-done | bytes 2097168 | tf_op jit(solution)/shard_map/while/body/eval_jaxpr/all_gather | solution.py:167
  242.1 38.2 %reduce-scatter.7.cloned.1.call-done = bf16[256,1024]{1,0:T(8,128)(2,1)} async-done(((bf16[1024,1024]{1,0:T(8,128)(2,1)}), bf16[256,1024]{1,0:T(8,128)(2,1)}) %reduce-scatter.7.cloned.1.call-update) | async-done | bytes 524304 | tf_op jit(solution)/shard_map/while/body/eval_jaxpr/reduce_scatter | solution.py:172
  301.7 46.6 %all-gather.5.cloned.1.call-done = bf16[1024,1024]{1,0:T(8,128)(2,1)} async-done(((bf16[256,1024]{1,0:T(8,128)(2,1)}), bf16[1024,1024]{1,0:T(8,128)(2,1)}) %all-gather.5.cloned.1.call-update) | async-done | bytes 2097168 | tf_op jit(solution)/shard_map/while/body/eval_jaxpr/all_gather | solution.py:146
  353.9 22.0 %while.124 = (s32[]{:T(128)}, bf16[2,512,4,64]{1,3,2,0:T(8,128)(2,1)S(1)}, f32[2,4,512]{2,1,0:T(4,128)S(1)}, s32[2]{0:T(128)S(1)}, bf16[1024,4,64]{0,2,1:T(8,128...) while((s32[]{:T(128)}, ...), condition=%wide.region_6.6_spmd, body=%wide.region_3.5_spmd.sunk | while | flops 562559488 | bytes 31264968 | solution.py:57
  379.2 75.6 %reduce-scatter.5.cloned.1.call-done = f32[256,1024]{1,0:T(8,128)} async-done(((f32[1024,1024]{1,0:T(8,128)}), f32[256,1024]{1,0:T(8,128)}) %reduce-scatter.5.cloned.1.call-update) | async-done | bytes 1048592 | tf_op jit(solution)/shard_map/while/body/eval_jaxpr/reduce_scatter | solution.py:158
  458.8 46.5 %all-gather.7.cloned.1.call-done = bf16[1024,1024]{1,0:T(8,128)(2,1)} async-done(((bf16[256,1024]{1,0:T(8,128)(2,1)}), bf16[1024,1024]{1,0:T(8,128)(2,1)}) %all-gather.7.cloned.1.call-update) | async-done | bytes 2097168 | tf_op jit(solution)/shard_map/while/body/eval_jaxpr/all_gather | solution.py:167
  520.9 38.1 %reduce-scatter.7.cloned.1.call-done = bf16[256,1024]{1,0:T(8,128)(2,1)} async-done(((bf16[1024,1024]{1,0:T(8,128)(2,1)}), bf16[256,1024]{1,0:T(8,128)(2,1)}) %reduce-scatter.7.cloned.1.call-update) | async-done | bytes 524304 | tf_op jit(solution)/shard_map/while/body/eval_jaxpr/reduce_scatter | solution.py:172
  580.4 46.6 %all-gather.5.cloned.1.call-done = bf16[1024,1024]{1,0:T(8,128)(2,1)} async-done(((bf16[256,1024]{1,0:T(8,128)(2,1)}), bf16[1024,1024]{1,0:T(8,128)(2,1)}) %all-gather.5.cloned.1.call-update) | async-done | bytes 2097168 | tf_op jit(solution)/shard_map/while/body/eval_jaxpr/all_gather | solution.py:146
  632.5 22.0 %while.124 = (s32[]{:T(128)}, bf16[2,512,4,64]{1,3,2,0:T(8,128)(2,1)S(1)}, f32[2,4,512]{2,1,0:T(4,128)S(1)}, s32[2]{0:T(128)S(1)}, bf16[1024,4,64]{0,2,1:T(8,128...) while((s32[]{:T(128)}, ...), condition=%wide.region_6.6_spmd, body=%wide.region_3.5_spmd.sunk | while | flops 562559488 | bytes 31264968 | solution.py:57
  657.9 75.6 %reduce-scatter.5.cloned.1.call-done = f32[256,1024]{1,0:T(8,128)} async-done(((f32[1024,1024]{1,0:T(8,128)}), f32[256,1024]{1,0:T(8,128)}) %reduce-scatter.5.cloned.1.call-update) | async-done | bytes 1048592 | tf_op jit(solution)/shard_map/while/body/eval_jaxpr/reduce_scatter | solution.py:158
  737.5 46.6 %all-gather.7.cloned.1.call-done = bf16[1024,1024]{1,0:T(8,128)(2,1)} async-done(((bf16[256,1024]{1,0:T(8,128)(2,1)}), bf16[1024,1024]{1,0:T(8,128)(2,1)}) %all-gather.7.cloned.1.call-update) | async-done | bytes 2097168 | tf_op jit(solution)/shard_map/while/body/eval_jaxpr/all_gather | solution.py:167
  799.5 38.2 %reduce-scatter.7.cloned.1.call-done = bf16[256,1024]{1,0:T(8,128)(2,1)} async-done(((bf16[1024,1024]{1,0:T(8,128)(2,1)}), bf16[256,1024]{1,0:T(8,128)(2,1)}) %reduce-scatter.7.cloned.1.call-update) | async-done | bytes 524304 | tf_op jit(solution)/shard_map/while/body/eval_jaxpr/reduce_scatter | solution.py:172
  854.4 8.4 constant_dynamic-slice_fusion.8
  877.5 907.6 %while.123 = (s32[]{:T(128)}, bf16[256,1024]{1,0:T(8,128)(2,1)S(1)}, f32[1024,768]{1,0:T(8,128)}, f32[2,256]{1,0:T(2,128)}, f32[256,1024]{1,0:T(8,128)}, /*index...) while((s32[]{:T(128)}, bf16[256,1024]{1,0:T(8,128)(2,1)S(1)}, ...), condition=%wide.region_34.35_spmd.clone, body=%wide.region_12.34_spmd.clone.sunk | while | flops 14322247680 | bytes 384561376 | solution.py:323
  900.9 46.6 %all-gather.9.cloned.1.call-done = bf16[1024,1024]{1,0:T(8,128)(2,1)} async-done(((bf16[256,1024]{1,0:T(8,128)(2,1)}), bf16[1024,1024]{1,0:T(8,128)(2,1)}) %all-gather.9.cloned.1.call-update) | async-done | bytes 2097168 | tf_op jit(solution)/shard_map/while/body/eval_jaxpr/all_gather | solution.py:228
  947.5 8.2 convert_reduce_fusion.13
  961.3 42.3 %reduce-scatter.9.cloned.1.call-done = bf16[256,1024]{1,0:T(8,128)(2,1)} async-done(((bf16[1024,1024]{1,0:T(8,128)(2,1)}), bf16[256,1024]{1,0:T(8,128)(2,1)}) %reduce-scatter.9.cloned.1.call-update) | async-done | bytes 524304 | tf_op jit(solution)/shard_map/while/body/eval_jaxpr/reduce_scatter | solution.py:239
  1010.4 43.6 %all-gather.11.cloned.1.call-done = bf16[1024,1024]{1,0:T(8,128)(2,1)} async-done(((bf16[256,1024]{1,0:T(8,128)(2,1)}), bf16[1024,1024]{1,0:T(8,128)(2,1)}) %all-gather.11.cloned.1.call-update) | async-done | bytes 2097168 | tf_op jit(solution)/shard_map/while/body/eval_jaxpr/all_gather | solution.py:252
  1057.2 65.4 %while.125 = (s32[]{:T(128)}, f32[1024,4,64]{0,2,1:T(8,128)S(1)}, f32[1024,4,64]{0,2,1:T(8,128)}, bf16[2,512,4,64]{1,0,3,2:T(2,128)(2,1)}, s32[2]{0:T(128)S(1)},...) while((s32[]{:T(128)}, f32[1024,4,64]{0,2,1:T(8,128)S(1)}, ...), condition=%wide.region_20.20_spmd.clone, body=%wide.region_18.19_spmd.clone.sunk | while | flops 1375730176 | bytes 161280368 | solution.py:98
  1079.5 9.8 dynamic_update_slice.106
  1112.8 9.8 dynamic_update_slice.106
  1149.8 22.9 %reduce-scatter.11.cloned.1.call-done = bf16[256,1024]{1,0:T(8,128)(2,1)} async-done(((bf16[1024,1024]{1,0:T(8,128)(2,1)}), bf16[256,1024]{1,0:T(8,128)(2,1)}) %reduce-scatter.11.cloned.1.call-update) | async-done | bytes 524304 | tf_op jit(solution)/shard_map/while/body/eval_jaxpr/reduce_scatter | solution.py:281
  1181.3 13.2 collective-permute-done
  1198.0 44.7 %all-gather.9.cloned.1.call-done = bf16[1024,1024]{1,0:T(8,128)(2,1)} async-done(((bf16[256,1024]{1,0:T(8,128)(2,1)}), bf16[1024,1024]{1,0:T(8,128)(2,1)}) %all-gather.9.cloned.1.call-update) | async-done | bytes 2097168 | tf_op jit(solution)/shard_map/while/body/eval_jaxpr/all_gather | solution.py:228
  1242.7 8.2 convert_reduce_fusion.13
  1256.5 42.3 %reduce-scatter.9.cloned.1.call-done = bf16[256,1024]{1,0:T(8,128)(2,1)} async-done(((bf16[1024,1024]{1,0:T(8,128)(2,1)}), bf16[256,1024]{1,0:T(8,128)(2,1)}) %reduce-scatter.9.cloned.1.call-update) | async-done | bytes 524304 | tf_op jit(solution)/shard_map/while/body/eval_jaxpr/reduce_scatter | solution.py:239
  1305.6 43.6 %all-gather.11.cloned.1.call-done = bf16[1024,1024]{1,0:T(8,128)(2,1)} async-done(((bf16[256,1024]{1,0:T(8,128)(2,1)}), bf16[1024,1024]{1,0:T(8,128)(2,1)}) %all-gather.11.cloned.1.call-update) | async-done | bytes 2097168 | tf_op jit(solution)/shard_map/while/body/eval_jaxpr/all_gather | solution.py:252
  1352.3 65.4 %while.125 = (s32[]{:T(128)}, f32[1024,4,64]{0,2,1:T(8,128)S(1)}, f32[1024,4,64]{0,2,1:T(8,128)}, bf16[2,512,4,64]{1,0,3,2:T(2,128)(2,1)}, s32[2]{0:T(128)S(1)},...) while((s32[]{:T(128)}, f32[1024,4,64]{0,2,1:T(8,128)S(1)}, ...), condition=%wide.region_20.20_spmd.clone, body=%wide.region_18.19_spmd.clone.sunk | while | flops 1375730176 | bytes 161280368 | solution.py:98
  1374.7 9.8 dynamic_update_slice.106
  1408.0 9.8 dynamic_update_slice.106
  1433.4 8.1 select_add_fusion.17
  1448.5 19.4 %reduce-scatter.11.cloned.1.call-done = bf16[256,1024]{1,0:T(8,128)(2,1)} async-done(((bf16[1024,1024]{1,0:T(8,128)(2,1)}), bf16[256,1024]{1,0:T(8,128)(2,1)}) %reduce-scatter.11.cloned.1.call-update) | async-done | bytes 524304 | tf_op jit(solution)/shard_map/while/body/eval_jaxpr/reduce_scatter | solution.py:281
  1476.5 13.2 collective-permute-done
  1493.2 44.7 %all-gather.9.cloned.1.call-done = bf16[1024,1024]{1,0:T(8,128)(2,1)} async-done(((bf16[256,1024]{1,0:T(8,128)(2,1)}), bf16[1024,1024]{1,0:T(8,128)(2,1)}) %all-gather.9.cloned.1.call-update) | async-done | bytes 2097168 | tf_op jit(solution)/shard_map/while/body/eval_jaxpr/all_gather | solution.py:228
  1537.9 8.2 convert_reduce_fusion.13
  1551.6 42.3 %reduce-scatter.9.cloned.1.call-done = bf16[256,1024]{1,0:T(8,128)(2,1)} async-done(((bf16[1024,1024]{1,0:T(8,128)(2,1)}), bf16[256,1024]{1,0:T(8,128)(2,1)}) %reduce-scatter.9.cloned.1.call-update) | async-done | bytes 524304 | tf_op jit(solution)/shard_map/while/body/eval_jaxpr/reduce_scatter | solution.py:239
  1600.8 43.6 %all-gather.11.cloned.1.call-done = bf16[1024,1024]{1,0:T(8,128)(2,1)} async-done(((bf16[256,1024]{1,0:T(8,128)(2,1)}), bf16[1024,1024]{1,0:T(8,128)(2,1)}) %all-gather.11.cloned.1.call-update) | async-done | bytes 2097168 | tf_op jit(solution)/shard_map/while/body/eval_jaxpr/all_gather | solution.py:252
  1647.5 65.4 %while.125 = (s32[]{:T(128)}, f32[1024,4,64]{0,2,1:T(8,128)S(1)}, f32[1024,4,64]{0,2,1:T(8,128)}, bf16[2,512,4,64]{1,0,3,2:T(2,128)(2,1)}, s32[2]{0:T(128)S(1)},...) while((s32[]{:T(128)}, f32[1024,4,64]{0,2,1:T(8,128)S(1)}, ...), condition=%wide.region_20.20_spmd.clone, body=%wide.region_18.19_spmd.clone.sunk | while | flops 1375730176 | bytes 161280368 | solution.py:98
  1669.9 9.8 dynamic_update_slice.106
  1703.1 9.8 dynamic_update_slice.106
  1743.6 19.4 %reduce-scatter.11.cloned.1.call-done = bf16[256,1024]{1,0:T(8,128)(2,1)} async-done(((bf16[1024,1024]{1,0:T(8,128)(2,1)}), bf16[256,1024]{1,0:T(8,128)(2,1)}) %reduce-scatter.11.cloned.1.call-update) | async-done | bytes 524304 | tf_op jit(solution)/shard_map/while/body/eval_jaxpr/reduce_scatter | solution.py:281
  1771.7 13.2 collective-permute-done
  1804.6 61.0 %all-reduce = (f32[1,1024]{1,0:T(1,128)}, f32[1,1024]{1,0:T(1,128)}, f32[1,1024]{1,0:T(1,128)}, f32[1,1024]{1,0:T(1,128)}, f32[1,1024]{1,0:T(1,128)}, /*index=5*/f32[1,1024]{1,0:T(1,128)}) all-reduce(f32[1,1024]{1,0:T(1,128)S(1)} %bitcast.361, ...), channel_id=1, replica_groups=mesh['section'=2,'tensor'=4,'dp'=4] {'tensor','dp'}, use_global_device_ids=true, to_apply=%region_35.36 | all-reduce | flops 6144 | bytes 49152 | tf_op jit(solution)/shard_map/psum | solution.py:343
  1867.7 49.1 %all-reduce.5.cloned.1.call-done = (bf16[1,1024,3,256]{1,3,2,0:T(8,128)(2,1)}, bf16[1,256,1024]{2,1,0:T(8,128)(2,1)}, bf16[1,1024,1024]{2,1,0:T(8,128)(2,1)}, bf16[1,1024,1024]{2,1,0:T(8,128)(2,1)}) async-done(((bf16[1,1024,3,256]{1,3,2,0:T(8,128)(2,1)}, bf16[1,256,1024]{2,1,0:T(8,128)(2,1)}, bf16[1,1024,1024]{2,1,0:T(8,128)(2,1)}, bf16[1,1024,1024]{2,1,0:T(8,128)(2,1)}), ...) | async-done | bytes 6291472 | tf_op jit(solution)/shard_map/psum | solution.py:329
  (784 shorter events, 538.2 us)
Async XLA Ops:
  15.9 53.7 %copy-start.28 = (bf16[1024,768]{1,0:T(8,128)(2,1)S(1)}, bf16[1024,768]{1,0:T(8,128)(2,1)}, u32[]{:S(2)}) copy-start(bf16[1024,768]{1,0:T(8,128)(2,1)} %get-tuple-element.2032) | copy-start | bytes 4718596 | tf_op jit(solution)/shard_map/while
  15.9 53.7 %all-gather.5.cloned.1.call-start = ((), (), s32[]{:S(2)}) async-start(), calls=%async_computation.5 | async-start | bytes 2621440 | tf_op jit(solution)/shard_map/while/body/eval_jaxpr/all_gather | solution.py:146
  20.8 155.3 %reduce-scatter.5.cloned.1.call-start = ((), (), s32[]{:S(2)}) async-start(), calls=%async_computation.6 | async-start | bytes 5242880 | tf_op jit(solution)/shard_map/while/body/eval_jaxpr/reduce_scatter | solution.py:158
  100.5 126.2 %all-gather.7.cloned.1.call-start = ((), (), s32[]{:S(2)}) async-start(), calls=%async_computation.7 | async-start | bytes 2621440 | tf_op jit(solution)/shard_map/while/body/eval_jaxpr/all_gather | solution.py:167
  180.1 100.2 %reduce-scatter.7.cloned.1.call-start = ((), (), s32[]{:S(2)}) async-start(), calls=%async_computation.8 | async-start | bytes 2621440 | tf_op jit(solution)/shard_map/while/body/eval_jaxpr/reduce_scatter | solution.py:172
  282.4 14.4 collective-permute-start.1
  296.8 51.5 %copy-start.28 = (bf16[1024,768]{1,0:T(8,128)(2,1)S(1)}, bf16[1024,768]{1,0:T(8,128)(2,1)}, u32[]{:S(2)}) copy-start(bf16[1024,768]{1,0:T(8,128)(2,1)} %get-tuple-element.2032) | copy-start | bytes 4718596 | tf_op jit(solution)/shard_map/while
  296.8 51.5 %all-gather.5.cloned.1.call-start = ((), (), s32[]{:S(2)}) async-start(), calls=%async_computation.5 | async-start | bytes 2621440 | tf_op jit(solution)/shard_map/while/body/eval_jaxpr/all_gather | solution.py:146
  301.6 153.2 %reduce-scatter.5.cloned.1.call-start = ((), (), s32[]{:S(2)}) async-start(), calls=%async_computation.6 | async-start | bytes 5242880 | tf_op jit(solution)/shard_map/while/body/eval_jaxpr/reduce_scatter | solution.py:158
  379.2 126.2 %all-gather.7.cloned.1.call-start = ((), (), s32[]{:S(2)}) async-start(), calls=%async_computation.7 | async-start | bytes 2621440 | tf_op jit(solution)/shard_map/while/body/eval_jaxpr/all_gather | solution.py:167
  458.8 100.2 %reduce-scatter.7.cloned.1.call-start = ((), (), s32[]{:S(2)}) async-start(), calls=%async_computation.8 | async-start | bytes 2621440 | tf_op jit(solution)/shard_map/while/body/eval_jaxpr/reduce_scatter | solution.py:172
  561.1 14.4 collective-permute-start.1
  575.5 51.5 %copy-start.28 = (bf16[1024,768]{1,0:T(8,128)(2,1)S(1)}, bf16[1024,768]{1,0:T(8,128)(2,1)}, u32[]{:S(2)}) copy-start(bf16[1024,768]{1,0:T(8,128)(2,1)} %get-tuple-element.2032) | copy-start | bytes 4718596 | tf_op jit(solution)/shard_map/while
  575.5 51.5 %all-gather.5.cloned.1.call-start = ((), (), s32[]{:S(2)}) async-start(), calls=%async_computation.5 | async-start | bytes 2621440 | tf_op jit(solution)/shard_map/while/body/eval_jaxpr/all_gather | solution.py:146
  580.4 153.1 %reduce-scatter.5.cloned.1.call-start = ((), (), s32[]{:S(2)}) async-start(), calls=%async_computation.6 | async-start | bytes 5242880 | tf_op jit(solution)/shard_map/while/body/eval_jaxpr/reduce_scatter | solution.py:158
  657.8 126.2 %all-gather.7.cloned.1.call-start = ((), (), s32[]{:S(2)}) async-start(), calls=%async_computation.7 | async-start | bytes 2621440 | tf_op jit(solution)/shard_map/while/body/eval_jaxpr/all_gather | solution.py:167
  737.4 100.2 %reduce-scatter.7.cloned.1.call-start = ((), (), s32[]{:S(2)}) async-start(), calls=%async_computation.8 | async-start | bytes 2621440 | tf_op jit(solution)/shard_map/while/body/eval_jaxpr/reduce_scatter | solution.py:172
  839.7 14.4 collective-permute-start.1
  897.4 58.3 %copy-start.64 = (s32[3]{0:T(128)}, s32[3]{0:T(128)S(1)}, u32[]{:S(2)}) copy-start(s32[3]{0:T(128)S(1)} %get-tuple-element.2146) | copy-start | bytes 40 | tf_op jit(solution)/shard_map/while
  897.4 107.6 %copy-start.3 = (f32[2,256,1024]{2,1,0:T(8,128)}, f32[2,256,1024]{2,1,0:T(8,128)S(1)}, u32[]{:S(2)}) copy-start(f32[2,256,1024]{2,1,0:T(8,128)S(1)} %get-tuple-element.2153) | copy-start | bytes 6291460 | tf_op jit(solution)/shard_map/while
  897.4 156.6 %copy-start.17 = (bf16[256,1024]{1,0:T(8,128)(2,1)}, bf16[256,1024]{1,0:T(8,128)(2,1)S(1)}, u32[]{:S(2)}) copy-start(bf16[256,1024]{1,0:T(8,128)(2,1)S(1)} %get-tuple-element.2156) | copy-start | bytes 1572868 | tf_op jit(solution)/shard_map/while
  897.5 50.0 %all-gather.9.cloned.1.call-start = ((), (), s32[]{:S(2)}) async-start(), calls=%async_computation.9 | async-start | bytes 2621440 | tf_op jit(solution)/shard_map/while/body/eval_jaxpr/all_gather | solution.py:228
  900.8 102.7 %reduce-scatter.9.cloned.1.call-start = ((), (), s32[]{:S(2)}) async-start(), calls=%async_computation.10 | async-start | bytes 2621440 | tf_op jit(solution)/shard_map/while/body/eval_jaxpr/reduce_scatter | solution.py:239
  960.8 46.7 %copy-start.7 = (bf16[256,1024]{1,0:T(8,128)(2,1)S(1)}, bf16[256,1024]{1,0:T(8,128)(2,1)}, u32[]{:S(2)}) copy-start(bf16[256,1024]{1,0:T(8,128)(2,1)} %bitcast_select_fusion.4) | copy-start | bytes 1572868 | tf_op jit(solution)/shard_map/while
  960.8 93.2 %all-gather.11.cloned.1.call-start = ((), (), s32[]{:S(2)}) async-start(), calls=%async_computation.11 | async-start | bytes 2621440 | tf_op jit(solution)/shard_map/while/body/eval_jaxpr/all_gather | solution.py:252
  1008.6 164.1 %reduce-scatter.11.cloned.1.call-start = ((), (), s32[]{:S(2)}) async-start(), calls=%async_computation.12 | async-start | bytes 2621440 | tf_op jit(solution)/shard_map/while/body/eval_jaxpr/reduce_scatter | solution.py:281
  1179.0 15.5 collective-permute-start
  1194.5 56.4 %copy-start.64 = (s32[3]{0:T(128)}, s32[3]{0:T(128)S(1)}, u32[]{:S(2)}) copy-start(s32[3]{0:T(128)S(1)} %get-tuple-element.2146) | copy-start | bytes 40 | tf_op jit(solution)/shard_map/while
  1194.5 105.6 %copy-start.3 = (f32[2,256,1024]{2,1,0:T(8,128)}, f32[2,256,1024]{2,1,0:T(8,128)S(1)}, u32[]{:S(2)}) copy-start(f32[2,256,1024]{2,1,0:T(8,128)S(1)} %get-tuple-element.2153) | copy-start | bytes 6291460 | tf_op jit(solution)/shard_map/while
  1194.6 154.6 %copy-start.17 = (bf16[256,1024]{1,0:T(8,128)(2,1)}, bf16[256,1024]{1,0:T(8,128)(2,1)S(1)}, u32[]{:S(2)}) copy-start(bf16[256,1024]{1,0:T(8,128)(2,1)S(1)} %get-tuple-element.2156) | copy-start | bytes 1572868 | tf_op jit(solution)/shard_map/while
  1194.6 48.1 %all-gather.9.cloned.1.call-start = ((), (), s32[]{:S(2)}) async-start(), calls=%async_computation.9 | async-start | bytes 2621440 | tf_op jit(solution)/shard_map/while/body/eval_jaxpr/all_gather | solution.py:228
  1198.0 100.8 %reduce-scatter.9.cloned.1.call-start = ((), (), s32[]{:S(2)}) async-start(), calls=%async_computation.10 | async-start | bytes 2621440 | tf_op jit(solution)/shard_map/while/body/eval_jaxpr/reduce_scatter | solution.py:239
  1256.0 46.7 %copy-start.7 = (bf16[256,1024]{1,0:T(8,128)(2,1)S(1)}, bf16[256,1024]{1,0:T(8,128)(2,1)}, u32[]{:S(2)}) copy-start(bf16[256,1024]{1,0:T(8,128)(2,1)} %bitcast_select_fusion.4) | copy-start | bytes 1572868 | tf_op jit(solution)/shard_map/while
  1256.0 93.2 %all-gather.11.cloned.1.call-start = ((), (), s32[]{:S(2)}) async-start(), calls=%async_computation.11 | async-start | bytes 2621440 | tf_op jit(solution)/shard_map/while/body/eval_jaxpr/all_gather | solution.py:252
  1303.8 164.1 %reduce-scatter.11.cloned.1.call-start = ((), (), s32[]{:S(2)}) async-start(), calls=%async_computation.12 | async-start | bytes 2621440 | tf_op jit(solution)/shard_map/while/body/eval_jaxpr/reduce_scatter | solution.py:281
  1474.1 15.5 collective-permute-start
  1489.7 56.4 %copy-start.64 = (s32[3]{0:T(128)}, s32[3]{0:T(128)S(1)}, u32[]{:S(2)}) copy-start(s32[3]{0:T(128)S(1)} %get-tuple-element.2146) | copy-start | bytes 40 | tf_op jit(solution)/shard_map/while
  1489.7 105.7 %copy-start.3 = (f32[2,256,1024]{2,1,0:T(8,128)}, f32[2,256,1024]{2,1,0:T(8,128)S(1)}, u32[]{:S(2)}) copy-start(f32[2,256,1024]{2,1,0:T(8,128)S(1)} %get-tuple-element.2153) | copy-start | bytes 6291460 | tf_op jit(solution)/shard_map/while
  1489.7 154.6 %copy-start.17 = (bf16[256,1024]{1,0:T(8,128)(2,1)}, bf16[256,1024]{1,0:T(8,128)(2,1)S(1)}, u32[]{:S(2)}) copy-start(bf16[256,1024]{1,0:T(8,128)(2,1)S(1)} %get-tuple-element.2156) | copy-start | bytes 1572868 | tf_op jit(solution)/shard_map/while
  1489.7 48.1 %all-gather.9.cloned.1.call-start = ((), (), s32[]{:S(2)}) async-start(), calls=%async_computation.9 | async-start | bytes 2621440 | tf_op jit(solution)/shard_map/while/body/eval_jaxpr/all_gather | solution.py:228
  1493.1 100.8 %reduce-scatter.9.cloned.1.call-start = ((), (), s32[]{:S(2)}) async-start(), calls=%async_computation.10 | async-start | bytes 2621440 | tf_op jit(solution)/shard_map/while/body/eval_jaxpr/reduce_scatter | solution.py:239
  1551.1 46.7 %copy-start.7 = (bf16[256,1024]{1,0:T(8,128)(2,1)S(1)}, bf16[256,1024]{1,0:T(8,128)(2,1)}, u32[]{:S(2)}) copy-start(bf16[256,1024]{1,0:T(8,128)(2,1)} %bitcast_select_fusion.4) | copy-start | bytes 1572868 | tf_op jit(solution)/shard_map/while
  1551.2 93.2 %all-gather.11.cloned.1.call-start = ((), (), s32[]{:S(2)}) async-start(), calls=%async_computation.11 | async-start | bytes 2621440 | tf_op jit(solution)/shard_map/while/body/eval_jaxpr/all_gather | solution.py:252
  1598.9 164.1 %reduce-scatter.11.cloned.1.call-start = ((), (), s32[]{:S(2)}) async-start(), calls=%async_computation.12 | async-start | bytes 2621440 | tf_op jit(solution)/shard_map/while/body/eval_jaxpr/reduce_scatter | solution.py:281
  1769.3 15.5 collective-permute-start
  1785.1 131.8 %all-reduce.5.cloned.1.call-start = ((), (), s32[]{:S(2)}) async-start(), calls=%async_computation.4 | async-start | bytes 12582912 | tf_op jit(solution)/shard_map/psum | solution.py:329
  1796.9 68.7 %copy-start.22 = (bf16[3,256,1024]{2,1,0:T(8,128)(2,1)S(1)}, bf16[3,256,1024]{2,1,0:T(8,128)(2,1)}, u32[]{:S(2)}) copy-start(bf16[3,256,1024]{2,1,0:T(8,128)(2,1)} %get-tuple-element.814) | copy-start | bytes 4718596
  1796.9 69.8 %copy-start.21 = (bf16[3,256,1024]{2,1,0:T(8,128)(2,1)S(1)}, bf16[3,256,1024]{2,1,0:T(8,128)(2,1)}, u32[]{:S(2)}) copy-start(bf16[3,256,1024]{2,1,0:T(8,128)(2,1)} %get-tuple-element.823) | copy-start | bytes 4718596
  (154 other events, 1141.8 us)
Sparse Core Ops, SparseCore 0:
  21.0 48.6 all-gather.4
  100.7 75.4 reduce-scatter.4
  180.2 46.4 all-gather.6
  237.7 42.5 reduce-scatter.6
  301.8 46.4 all-gather.4
  379.3 75.4 reduce-scatter.4
  458.9 46.4 all-gather.6
  516.4 42.5 reduce-scatter.6
  580.5 46.4 all-gather.4
  658.0 75.4 reduce-scatter.4
  737.5 46.4 all-gather.6
  795.0 42.5 reduce-scatter.6
  901.0 46.4 all-gather.8
  960.9 42.5 reduce-scatter.8
  1008.7 45.2 all-gather.10
  1130.1 42.5 reduce-scatter.10
  1198.1 44.5 all-gather.8
  1256.1 42.5 reduce-scatter.8
  1303.9 45.2 all-gather.10
  1425.3 42.5 reduce-scatter.10
  1493.2 44.5 all-gather.8
  1551.3 42.5 reduce-scatter.8
  1599.1 45.2 all-gather.10
  1720.5 42.5 reduce-scatter.10
Sparse Core Ops, SparseCore 1:
  1797.0 119.8 all-reduce.4
where the time goes:
time: 1950 us; the launch traced here: 1930 us
  waiting for transfers between devices  1190 us (61%)
  matrix products  287 us (15%)
  local copies, waits for them, and re-layouts  168 us (9%)
  other arithmetic  138 us (7%)
  blocking collectives  66.9 us (3%)
  loops' own time  52 us (3%)
    reduce_scatter x3, waiting for transfers between devices, forward_tick(): lax.psum_scatter(jnp.dot(blended, mixing_matrix, preferred_element_type=j...  227 us
    all_gather x3, waiting for transfers between devices, forward_tick(): normed_full = lax.all_gather(normed, 'tensor', axis=0, tiled=True)  142 us
    all_gather x3, waiting for transfers between devices, forward_tick(): feed_input = lax.all_gather(second, 'tensor', axis=0, tiled=True)  140 us
    all_gather x3, waiting for transfers between devices, backward_tick(): change_full = lax.all_gather(out_change, 'tensor', axis=0, tiled=True)  136 us
    all_gather x3, waiting for transfers between devices, backward_tick(): lax.all_gather(middle_change.astype(jnp.bfloat16), 'tensor', axis=0, tile...  131 us
    reduce_scatter x3, waiting for transfers between devices, backward_tick(): lax.psum_scatter(lax.dot_general(pre_change, expand_matrix, contract_last...  127 us
    reduce_scatter x3, waiting for transfers between devices, forward_tick(): lax.psum_scatter(lax.dot_general(hidden, shrink_matrix, contract_last, pr...  115 us
    ppermute x6, waiting for transfers between devices, from_behind(): return lax.ppermute(block, axis, route)  63 us
  transfers between devices with their start and end apart: 31, of which 31 were waited for; matrix products, arithmetic and copies ran while one was open for 5% of the time, Pallas kernels for 0%

commit v1 on v0

v1 whole, which is shorter than its diff:
```python
import jax
import jax.numpy as jnp
from jax import lax
from jax.experimental import pallas as pl
from jax.experimental.pallas import tpu as pltpu
from jax.sharding import PartitionSpec as P

HD = 64
PAIR = 2 * HD
BLOCK = 256


epsilon = 1e-05
contract_rows = (((0,), (0,)), ((), ()))
contract_last = (((1,), (1,)), ((), ()))


def dot(left, right, dims=(((1,), (0,)), ((), ()))):
    return lax.dot_general(left, right, dims, preferred_element_type=jnp.float32)


def layer_norm(values, gain_row, shift_row):
    center = values - jnp.mean(values, axis=-1, keepdims=True)
    spread = jnp.mean(center * center, axis=-1, keepdims=True)
    return center * lax.rsqrt(spread + epsilon) * gain_row + shift_row


def smooth_gate(values):
    return jax.nn.gelu(values, approximate=True)


def masked_scores(query_block, key_rows, row_first):
    scores = dot(query_block, key_rows, contract_last)
    row_ids = row_first + lax.broadcasted_iota(jnp.int32, scores.shape, 0)
    col_ids = lax.broadcasted_iota(jnp.int32, scores.shape, 1)
    return jnp.where(row_ids >= col_ids, scores, -jnp.inf)


def forward_kernel(query_ref, key_ref, value_ref, blended_ref, logsum_ref):
    length = query_ref.shape[0]
    block_rows = min(BLOCK, length)
    for head in range(2):
        lanes = slice(head * HD, (head + 1) * HD)
        for first in range(0, length, block_rows):
            rows = slice(first, first + block_rows)
            seen = slice(0, first + block_rows)
            query_block = query_ref[rows, lanes] * jnp.bfloat16(HD**-0.5)
            scores = masked_scores(query_block, key_ref[seen, lanes], first)
            largest = jnp.max(scores, axis=-1, keepdims=True)
            weights = jnp.exp(scores - largest)
            totals = jnp.sum(weights, axis=-1, keepdims=True)
            shares = (weights * (1.0 / totals)).astype(jnp.bfloat16)
            blended_ref[rows, lanes] = dot(shares, value_ref[seen, lanes]).astype(jnp.bfloat16)
            logsum_ref[rows, lanes] = jnp.broadcast_to(
                largest + jnp.log(totals), (block_rows, HD)
            )


def backward_kernel(
    query_ref,
    key_ref,
    value_ref,
    change_ref,
    logsum_ref,
    query_change_ref,
    key_change_ref,
    value_change_ref,
    key_sum,
    value_sum,
):
    length = query_ref.shape[0]
    block_rows = min(BLOCK, length)
    key_sum[...] = jnp.zeros_like(key_sum)
    value_sum[...] = jnp.zeros_like(value_sum)
    for head in range(2):
        lanes = slice(head * HD, (head + 1) * HD)
        for first in range(0, length, block_rows):
            rows = slice(first, first + block_rows)
            seen = slice(0, first + block_rows)
            query_block = query_ref[rows, lanes] * jnp.bfloat16(HD**-0.5)
            change_block = change_ref[rows, lanes]
            scores = masked_scores(query_block, key_ref[seen, lanes], first)
            shares = jnp.exp(scores - logsum_ref[rows, lanes][:, :1])
            share_change = dot(change_block, value_ref[seen, lanes], contract_last)
            row_inner = jnp.sum(share_change * shares, axis=-1, keepdims=True)
            score_change = (shares * (share_change - row_inner)).astype(jnp.bfloat16)
            query_change_ref[rows, lanes] = (
                dot(score_change, key_ref[seen, lanes]) * HD**-0.5
            ).astype(jnp.bfloat16)
            key_sum[seen, lanes] += dot(score_change, query_block, contract_rows)
            value_sum[seen, lanes] += dot(
                shares.astype(jnp.bfloat16), change_block, contract_rows
            )
    key_change_ref[...] = key_sum[...].astype(jnp.bfloat16)
    value_change_ref[...] = value_sum[...].astype(jnp.bfloat16)


def pair_spec(length, offset):
    return pl.BlockSpec((length, PAIR), lambda pair: (0, pair + offset))


def attend_forward(projected):
    length, width = projected.shape[0], projected.shape[1] // 3
    pairs = width // PAIR
    return pl.pallas_call(
        forward_kernel,
        grid=(pairs,),
        in_specs=[pair_spec(length, part * pairs) for part in range(3)],
        out_specs=[pair_spec(length, 0)] * 2,
        out_shape=[
            jax.ShapeDtypeStruct((length, width), jnp.bfloat16),
            jax.ShapeDtypeStruct((length, width), jnp.float32),
        ],
        compiler_params=pltpu.CompilerParams(vmem_limit_bytes=32 * 2**20),
        cost_estimate=pl.CostEstimate(
            flops=4 * length * length * width,
            bytes_accessed=12 * length * width,
            transcendentals=length * length * width // HD,
        ),
        name="attend_forward",
    )(projected, projected, projected)


def attend_backward(projected, change, logsum):
    length, width = projected.shape[0], projected.shape[1] // 3
    pairs = width // PAIR
    return pl.pallas_call(
        backward_kernel,
        grid=(pairs,),
        in_specs=[pair_spec(length, part * pairs) for part in range(3)]
        + [pair_spec(length, 0)] * 2,
        out_specs=[pair_spec(length, 0)] * 3,
        out_shape=[jax.ShapeDtypeStruct((length, width), jnp.bfloat16)] * 3,
        scratch_shapes=[pltpu.VMEM((length, PAIR), jnp.float32)] * 2,
        compiler_params=pltpu.CompilerParams(vmem_limit_bytes=32 * 2**20),
        cost_estimate=pl.CostEstimate(
            flops=10 * length * length * width,
            bytes_accessed=18 * length * width,
            transcendentals=length * length * width // HD,
        ),
        name="attend_backward",
    )(projected, projected, projected, change, logsum)


def gathered(block):
    return lax.all_gather(block, "tensor", axis=0, tiled=True)


def scattered(block):
    return lax.psum_scatter(
        block.astype(jnp.bfloat16), "tensor", scatter_dimension=0, tiled=True
    ).astype(jnp.float32)


def swapped(block):
    return lax.ppermute(block, "section", [(0, 1), (1, 0)])


def layer_forward(layer_input, weights):
    attend, mixing, expand, shrink, rows = weights
    gain_one, shift_one, mixing_offset, gain_two, shift_two, shrink_offset = rows[:6]
    attend_offset, expand_offset = rows[6:]
    residual = layer_input.astype(jnp.float32)
    normed = gathered(layer_norm(residual, gain_one, shift_one).astype(jnp.bfloat16))
    projected = (dot(normed, attend) + attend_offset).astype(jnp.bfloat16)
    blended, logsum = attend_forward(projected)
    middle = residual + scattered(dot(blended, mixing)) + mixing_offset
    feed = gathered(layer_norm(middle, gain_two, shift_two).astype(jnp.bfloat16))
    hidden_pre = dot(feed, expand) + expand_offset
    hidden = smooth_gate(hidden_pre).astype(jnp.bfloat16)
    branch = scattered(dot(hidden, shrink, contract_last))
    result = (middle + branch + shrink_offset).astype(jnp.bfloat16)
    return result, (layer_input, normed, projected, logsum, blended, middle, feed, hidden_pre)


def layer_backward(out_change, weights, kept):
    attend, mixing, expand, shrink, rows = weights
    gain_one, shift_one, mixing_offset, gain_two, shift_two, shrink_offset = rows[:6]
    layer_input, normed, projected, logsum, blended, middle, feed, hidden_pre = kept
    gate_value, gate_back = jax.vjp(smooth_gate, hidden_pre)
    hidden = gate_value.astype(jnp.bfloat16)
    change_full = gathered(out_change)
    shrink_change = dot(change_full, hidden, contract_rows).astype(jnp.bfloat16)
    pre_change = gate_back(dot(change_full, shrink))[0].astype(jnp.bfloat16)
    expand_change = dot(feed, pre_change, contract_rows).astype(jnp.bfloat16)
    expand_row_change = jnp.sum(pre_change.astype(jnp.float32), axis=0)
    second_change = scattered(dot(pre_change, expand, contract_last))
    middle_norm, gain_two_change, shift_two_change = jax.vjp(
        layer_norm, middle, gain_two, shift_two
    )[1](second_change)
    out_float = out_change.astype(jnp.float32)
    middle_change = out_float + middle_norm
    branch_full = gathered(middle_change.astype(jnp.bfloat16))
    mixing_change = dot(blended, branch_full, contract_rows).astype(jnp.bfloat16)
    blended_change = dot(branch_full, mixing, contract_last).astype(jnp.bfloat16)
    query_change, key_change, value_change = attend_backward(projected, blended_change, logsum)
    projected_change = jnp.concatenate([query_change, key_change, value_change], axis=1)
    attend_change = dot(normed, projected_change, contract_rows).astype(jnp.bfloat16)
    bias_change = jnp.concatenate(
        [
            jnp.sum(query_change.astype(jnp.float32), axis=0),
            jnp.sum(value_change.astype(jnp.float32), axis=0),
        ]
    )
    first_change = scattered(dot(projected_change, attend, contract_last))
    input_norm, gain_one_change, shift_one_change = jax.vjp(
        layer_norm, layer_input.astype(jnp.float32), gain_one, shift_one
    )[1](first_change)
    input_change = (middle_change + input_norm).astype(jnp.bfloat16)
    row_changes = jnp.stack(
        [
            gain_one_change,
            shift_one_change,
            jnp.sum(middle_change, axis=0),
            gain_two_change,
            shift_two_change,
            jnp.sum(out_float, axis=0),
        ]
    )
    column_changes = jnp.concatenate([bias_change, expand_row_change])
    return (
        input_change,
        (expand_change, shrink_change),
        (attend_change, mixing_change),
        row_changes,
        column_changes,
    )


def total(blocks, after=None):
    if after is not None:
        blocks, after = lax.optimization_barrier((blocks, after))
    sums = lax.psum(blocks, ("section", "dp"))
    return sums, after


def body(
    block_input,
    cotangent,
    first_gain,
    first_shift,
    attend_weight,
    attend_bias,
    mixing_weight,
    mixing_bias,
    second_gain,
    second_shift,
    expand_weight,
    expand_bias,
    shrink_weight,
    shrink_bias,
):
    micro_count, local_rows, model_width = block_input.shape
    local_width = attend_weight.shape[3]
    hidden_width = expand_weight.shape[2]
    section_index = lax.axis_index("section")
    early = section_index == 0

    small = jnp.concatenate(
        [
            first_gain[0],
            first_shift[0],
            mixing_bias[0],
            second_gain[0],
            second_shift[0],
            shrink_bias[0],
            attend_bias[0, 0],
            attend_bias[0, 1],
            expand_bias[0],
        ]
    )
    own = (
        attend_weight[0].reshape(model_width, 3 * local_width),
        mixing_weight[0],
        expand_weight[0],
        shrink_weight[0],
        small,
    )
    other = jax.tree.map(swapped, own)

    def weights_of(layer):
        attend, mixing, expand, shrink, row = (
            jnp.where(early == (layer == 0), mine, theirs) for mine, theirs in zip(own, other)
        )
        row = row.astype(jnp.float32)
        rows = [row[part * model_width : (part + 1) * model_width] for part in range(6)]
        row = row[6 * model_width :]
        blank = jnp.zeros((local_width,), jnp.float32)
        query_offset, value_offset = row[:local_width], row[local_width : 2 * local_width]
        rows.append(jnp.concatenate([query_offset, blank, value_offset]))
        rows.append(row[2 * local_width :])
        return attend, mixing, expand, shrink, rows

    weights = [weights_of(0), weights_of(1)]
    taken = lax.dynamic_index_in_dim(block_input, section_index, 0, keepdims=False)
    given = lax.dynamic_index_in_dim(cotangent, section_index, 0, keepdims=False)

    first_result, first_kept = layer_forward(taken, weights[0])
    second_result, second_kept = layer_forward(first_result, weights[1])
    second_back = layer_backward(given, weights[1], second_kept)
    first_back = layer_backward(second_back[0], weights[0], first_kept)

    def placed(first, second):
        mine = jnp.where(early, first, second)
        theirs = swapped(jnp.where(early, second, first))
        return jnp.stack([jnp.where(early, mine, theirs), jnp.where(early, theirs, mine)])[None]

    section_output = placed(first_result, second_result)
    input_changes = placed(first_back[0], second_back[0])

    late_wide, mark = total(second_back[1])
    late_narrow, mark = total(second_back[2], late_wide)
    soon_wide, mark = total(first_back[1], late_narrow)
    soon_narrow, mark = total(first_back[2], soon_wide)
    columns = lax.psum(jnp.stack([first_back[4], second_back[4]]), ("section", "dp"))
    rows = lax.psum(
        jnp.stack([first_back[3], second_back[3]]), ("section", "dp", "tensor")
    )

    def chosen(first, second):
        return jnp.where(early, first, second).astype(jnp.float32)

    expand_total = chosen(soon_wide[0], late_wide[0])
    shrink_total = chosen(soon_wide[1], late_wide[1])
    attend_total = chosen(soon_narrow[0], late_narrow[0])
    mixing_total = chosen(soon_narrow[1], late_narrow[1])
    column_total = chosen(columns[0], columns[1])
    row_total = chosen(rows[0], rows[1])
    return (
        section_output,
        input_changes,
        row_total[0:1],
        row_total[1:2],
        attend_total.reshape(1, model_width, 3, local_width),
        column_total[: 2 * local_width].reshape(1, 2, local_width),
        mixing_total[None],
        row_total[2:3],
        row_total[3:4],
        row_total[4:5],
        expand_total[None],
        column_total[2 * local_width :][None],
        shrink_total[None],
        row_total[5:6],
    )


def solution(mesh):
    placed = (
        P("dp", "tensor", None),
        P("dp", "tensor", None),
        P("section", None),
        P("section", None),
        P("section", None, None, "tensor"),
        P("section", None, "tensor"),
        P("section", "tensor", None),
        P("section", None),
        P("section", None),
        P("section", None),
        P("section", None, "tensor"),
        P("section", "tensor"),
        P("section", None, "tensor"),
        P("section", None),
    )
    return jax.shard_map(
        body,
        mesh=mesh,
        in_specs=placed,
        out_specs=(
            P("section", "dp", "tensor", None),
            P("section", "dp", "tensor", None),
            P("section", None),
            P("section", None),
            P("section", None, None, "tensor"),
            P("section", None, "tensor"),
            P("section", "tensor", None),
            P("section", None),
            P("section", None),
            P("section", None),
            P("section", None, "tensor"),
            P("section", "tensor"),
            P("section", None, "tensor"),
            P("section", None),
        ),
        check_vma=False,
    )
```

time: 1950 us -> 1260 us (0.65)
  waiting for transfers between devices: 1190 us -> 909 us
  matrix products: 287 us -> 108 us
  local copies, waits for them, and re-layouts: 168 us -> 30.6 us
  other arithmetic: 138 us -> 58.6 us
  loops' own time: 52 us -> 0 us
  Pallas kernels: 0 us -> 44.9 us
    all_gather x12 -> x8, waiting for transfers between devices: 548 us -> 252 us  [gathered(): return lax.all_gather(block, 'tensor', axis=0, tiled=True)]
    reduce_scatter x12 -> x8, waiting for transfers between devices: 530 us -> 334 us  [scattered(): lax.psum_scatter(block.astype(jnp.bfloat16), 'tensor', scatter_dimension=...]
    dot_general x78 -> x24, matrix products: 287 us -> 108 us  [dot(): lax.dot_general(left, right, dims, preferred_element_type=jnp.float32)]
    psum x1 -> x4, waiting for transfers between devices: 49.1 us -> 184 us  [total(): sums = lax.psum(blocks, ('section', 'dp'))]
    dynamic_update_slice x27 -> x0, local copies, waits for them, and re-layouts: 83 us -> none  [the longest x12 61.1 us: attend_forward(): blended, logsum = lax.map(one_block, firsts)]
    ppermute x6 -> x7, waiting for transfers between devices: 63 us -> 139 us  [swapped(): return lax.ppermute(block, 'section', [(0, 1), (1, 0)])]
    another operation x8 -> x0, loops' own time: 52 us -> none  [the longest x1 23.9 us: body(): lax.scan(backward_tick, (first_carry, zero_sums), tick_steps)]
    pallas_call x0 -> x4, Pallas kernels: none -> 44.9 us  [the longest x2 26.7 us: attend_backward(): pl.pallas_call(backward_kernel, grid=(pairs,), in_specs=[pair_spec(length...]
  transfers between devices with their start and end apart: 31 -> 27, of which waited for: 31 -> 23; matrix products, arithmetic and copies ran while one was open for 5% -> 9% of each run, Pallas kernels for 0% -> 2%
where the time goes in v1:
time: 1260 us; the launch traced here: 1250 us
  waiting for transfers between devices  909 us (72%)
  matrix products  108 us (9%)
  blocking collectives  68.1 us (5%)
  other arithmetic  58.6 us (5%)
  Pallas kernels  44.9 us (4%)
  local copies, waits for them, and re-layouts  30.6 us (2%)
  between operations  15.6 us (1%)
  starting transfers between devices  12.8 us (1%)
    reduce_scatter x8, waiting for transfers between devices, scattered(): lax.psum_scatter(block.astype(jnp.bfloat16), 'tensor', scatter_dimension=...  334 us
    all_gather x8, waiting for transfers between devices, gathered(): return lax.all_gather(block, 'tensor', axis=0, tiled=True)  252 us
    psum x4, waiting for transfers between devices, total(): sums = lax.psum(blocks, ('section', 'dp'))  184 us
    ppermute x7, waiting for transfers between devices, swapped(): return lax.ppermute(block, 'section', [(0, 1), (1, 0)])  139 us
    dot_general x24, matrix products, dot(): lax.dot_general(left, right, dims, preferred_element_type=jnp.float32)  108 us
    psum x1, blocking collectives, body(): lax.psum(jnp.stack([first_back[3], second_back[3]]), ('section', 'dp', 't...  45 us
    pallas_call x2, Pallas kernels, attend_backward(): pl.pallas_call(backward_kernel, grid=(pairs,), in_specs=[pair_spec(length...  26.7 us
  transfers between devices with their start and end apart: 27, of which 23 were waited for; matrix products, arithmetic and copies ran while one was open for 9% of the time, Pallas kernels for 2%

profile of v1, /device:TPU:0, one launch (start us, length us, event | category | flops | bytes accessed | tf_op | source)
XLA Modules:
  0.0 1247.6 jit_solution(12799965003100671409)
XLA Ops:
  27.5 35.5 %collective-permute-done.1 = bf16[1024,768]{1,0:T(8,128)(2,1)S(1)} collective-permute-done((bf16[1024,768]{1,0:T(8,128)(2,1)}, bf16[1024,768]{1,0:T(8,128)(2,1)S(1)}, u32[]{:S(2)}, u32[]{:S(2)}) %collective-permute-start.1) | collective-permute-done | bytes 1572896 | tf_op jit(solution)/shard_map/ppermute | solution.py:156
  62.9 5.5 all-gather.10.cloned.1.call-done
  68.4 3.8 add_convert_fusion.1.query_ref.key_ref.value_ref
  72.3 9.1 attend_forward.2
  84.5 42.2 %reduce-scatter.9.cloned.1.call-done = bf16[256,1024]{1,0:T(8,128)(2,1)} async-done(((bf16[1024,1024]{1,0:T(8,128)(2,1)}), bf16[256,1024]{1,0:T(8,128)(2,1)}) %reduce-scatter.9.cloned.1.call-update) | async-done | bytes 524304 | tf_op jit(solution)/shard_map/reduce_scatter | solution.py:150
  133.3 46.8 %collective-permute-done.3 = bf16[1024,1024]{1,0:T(8,128)(2,1)} collective-permute-done((bf16[1024,1024]{1,0:T(8,128)(2,1)}, bf16[1024,1024]{1,0:T(8,128)(2,1)}, u32[]{:S(2)}, u32[]{:S(2)}) %collective-permute-start.3) | collective-permute-done | bytes 2097184 | tf_op jit(solution)/shard_map/ppermute | solution.py:156
  180.1 4.7 fusion.62
  184.8 38.9 %collective-permute-done.4 = bf16[1024,1024]{1,0:T(8,128)(2,1)} collective-permute-done((bf16[1024,1024]{1,0:T(8,128)(2,1)}, bf16[1024,1024]{1,0:T(8,128)(2,1)}, u32[]{:S(2)}, u32[]{:S(2)}) %collective-permute-start.4) | collective-permute-done | bytes 2097184 | tf_op jit(solution)/shard_map/ppermute | solution.py:156
  223.7 4.2 convolution_convert_fusion.7
  228.0 45.1 %reduce-scatter.11.cloned.1.call-done = bf16[256,1024]{1,0:T(8,128)(2,1)} async-done(((bf16[1024,1024]{1,0:T(8,128)(2,1)}), bf16[256,1024]{1,0:T(8,128)(2,1)}) %reduce-scatter.11.cloned.1.call-update) | async-done | bytes 524304 | tf_op jit(solution)/shard_map/reduce_scatter | solution.py:150
  276.0 45.4 %all-gather.14.cloned.1.call-done = bf16[1024,1024]{1,0:T(8,128)(2,1)} async-done(((bf16[256,1024]{1,0:T(8,128)(2,1)}), bf16[1024,1024]{1,0:T(8,128)(2,1)}) %all-gather.14.cloned.1.call-update) | async-done | bytes 2097168 | tf_op jit(solution)/shard_map/all_gather | solution.py:146
  321.4 3.8 add_convert_fusion.query_ref.key_ref.value_ref
  325.2 9.1 attend_forward.3
  337.5 42.3 %reduce-scatter.13.cloned.1.call-done = bf16[256,1024]{1,0:T(8,128)(2,1)} async-done(((bf16[1024,1024]{1,0:T(8,128)(2,1)}), bf16[256,1024]{1,0:T(8,128)(2,1)}) %reduce-scatter.13.cloned.1.call-update) | async-done | bytes 524304 | tf_op jit(solution)/shard_map/reduce_scatter | solution.py:150
  385.9 43.1 %all-gather.16.cloned.1.call-done = bf16[1024,1024]{1,0:T(8,128)(2,1)} async-done(((bf16[256,1024]{1,0:T(8,128)(2,1)}), bf16[1024,1024]{1,0:T(8,128)(2,1)}) %all-gather.16.cloned.1.call-update) | async-done | bytes 2097168 | tf_op jit(solution)/shard_map/all_gather | solution.py:146
  429.0 7.2 fusion.64
  436.2 39.1 %all-gather.24.cloned.1.call-done = bf16[1,1024,1024]{2,1,0:T(8,128)(2,1)} async-done(((bf16[1,256,1024]{2,1,0:T(8,128)(2,1)}), bf16[1,1024,1024]{2,1,0:T(8,128)(2,1)}) %all-gather.24.cloned.1.call-update) | async-done | bytes 2097168 | tf_op jit(solution)/shard_map/all_gather | solution.py:146
  475.4 9.0 convert_reduce_fusion
  485.6 5.3 convolution_convert_fusion.4
  491.0 41.8 %reduce-scatter.17.cloned.1.call-done = bf16[256,1024]{1,0:T(8,128)(2,1)} async-done(((bf16[1024,1024]{1,0:T(8,128)(2,1)}), bf16[256,1024]{1,0:T(8,128)(2,1)}) %reduce-scatter.17.cloned.1.call-update) | async-done | bytes 524304 | tf_op jit(solution)/shard_map/reduce_scatter | solution.py:150
  538.8 45.1 %all-gather.18.cloned.1.call-done = bf16[1024,1024]{1,0:T(8,128)(2,1)} async-done(((bf16[256,1024]{1,0:T(8,128)(2,1)}), bf16[1024,1024]{1,0:T(8,128)(2,1)}) %all-gather.18.cloned.1.call-update) | async-done | bytes 2097168 | tf_op jit(solution)/shard_map/all_gather | solution.py:146
  588.9 13.3 %attend_backward.2 = (bf16[1024,256]{1,0:T(8,128)(2,1)S(1)}, bf16[1024,256]{1,0:T(8,128)(2,1)S(1)}, bf16[1024,256]{1,0:T(8,128)(2,1)S(1)}) custom-call(bf16[1024,768]{1,0:T(8,128)(2,1)S(1)} %copy-done.3, bf16[1024,768]{1,0:T(8,128)(2,1)S(1)} %copy-done.3, bf16[1024,768]{1,0:T(8,128)(2,1)S(1)} %copy-done.3, ...), custom_call_target="tpu_custom_call" | custom-call | flops 2684354560 | bytes 4718592 | tf_op jit(solution)/shard_map/attend_backward/pallas_call | solution.py:127
  607.9 42.7 %reduce-scatter.19.cloned.1.call-done = bf16[256,1024]{1,0:T(8,128)(2,1)} async-done(((bf16[1024,1024]{1,0:T(8,128)(2,1)}), bf16[256,1024]{1,0:T(8,128)(2,1)}) %reduce-scatter.19.cloned.1.call-update) | async-done | bytes 524304 | tf_op jit(solution)/shard_map/reduce_scatter | solution.py:150
  655.6 6.1 convolution_convert_fusion
  661.7 4.0 fusion.20
  665.8 34.8 %all-gather.20.cloned.1.call-done = bf16[1024,1024]{1,0:T(8,128)(2,1)} async-done(((bf16[256,1024]{1,0:T(8,128)(2,1)}), bf16[1024,1024]{1,0:T(8,128)(2,1)}) %all-gather.20.cloned.1.call-update) | async-done | bytes 2097168 | tf_op jit(solution)/shard_map/all_gather | solution.py:146
  700.6 8.3 convert_reduce_fusion.1
  710.2 3.7 convolution_convert_fusion.3
  717.5 4.7 convolution_convert_fusion.11
  722.2 62.0 %all-reduce.15.cloned.1.call-done = (bf16[1024,1024]{1,0:T(8,128)(2,1)}, bf16[1024,1024]{1,0:T(8,128)(2,1)}) async-done(((bf16[1024,1024]{1,0:T(8,128)(2,1)}, bf16[1024,1024]{1,0:T(8,128)(2,1)}), (bf16[1024,1024]{1,0:T(8,128)(2,1)}, bf16[1024,1024]{1,0:T(8,128)(2,1)})) %all-reduce.15.cloned.1.call-update) | async-done | bytes 4194320 | tf_op jit(solution)/shard_map/psum | solution.py:233
  784.3 46.6 %reduce-scatter.21.cloned.1.call-done = bf16[256,1024]{1,0:T(8,128)(2,1)} async-done(((bf16[1024,1024]{1,0:T(8,128)(2,1)}), bf16[256,1024]{1,0:T(8,128)(2,1)}) %reduce-scatter.21.cloned.1.call-update) | async-done | bytes 524304 | tf_op jit(solution)/shard_map/reduce_scatter | solution.py:150
  837.1 6.4 convolution_convert_fusion.2
  843.6 4.0 convolution_convert_fusion.1
  847.5 47.7 %all-reduce.13.cloned.1.call-done = (bf16[1024,768]{1,0:T(8,128)(2,1)}, bf16[256,1024]{1,0:T(8,128)(2,1)}) async-done(((bf16[1024,768]{1,0:T(8,128)(2,1)}, bf16[256,1024]{1,0:T(8,128)(2,1)}), (bf16[1024,768]{1,0:T(8,128)(2,1)}, bf16[256,1024]{1,0:T(8,128)(2,1)})) %all-reduce.13.cloned.1.call-update) | async-done | bytes 2097168 | tf_op jit(solution)/shard_map/psum | solution.py:233
  895.3 7.7 convolution_convert_fusion.5
  903.3 39.2 %all-gather.22.cloned.1.call-done = bf16[1024,1024]{1,0:T(8,128)(2,1)} async-done(((bf16[256,1024]{1,0:T(8,128)(2,1)}), bf16[1024,1024]{1,0:T(8,128)(2,1)}) %all-gather.22.cloned.1.call-update) | async-done | bytes 2097168 | tf_op jit(solution)/shard_map/all_gather | solution.py:146
  947.5 13.3 %attend_backward.3 = (bf16[1024,256]{1,0:T(8,128)(2,1)S(1)}, bf16[1024,256]{1,0:T(8,128)(2,1)S(1)}, bf16[1024,256]{1,0:T(8,128)(2,1)S(1)}) custom-call(bf16[1024,768]{1,0:T(8,128)(2,1)S(1)} %copy-done.1, bf16[1024,768]{1,0:T(8,128)(2,1)S(1)} %copy-done.1, bf16[1024,768]{1,0:T(8,128)(2,1)S(1)} %copy-done.1, ...), custom_call_target="tpu_custom_call" | custom-call | flops 2684354560 | bytes 4718592 | tf_op jit(solution)/shard_map/attend_backward/pallas_call | solution.py:127
  967.1 59.5 %all-reduce.11.cloned.1.call-done = (bf16[1024,1024]{1,0:T(8,128)(2,1)}, bf16[1024,1024]{1,0:T(8,128)(2,1)}) async-done(((bf16[1024,1024]{1,0:T(8,128)(2,1)}, bf16[1024,1024]{1,0:T(8,128)(2,1)}), (bf16[1024,1024]{1,0:T(8,128)(2,1)}, bf16[1024,1024]{1,0:T(8,128)(2,1)})) %all-reduce.11.cloned.1.call-update) | async-done | bytes 4194320 | tf_op jit(solution)/shard_map/psum | solution.py:233
  1026.9 5.1 convolution_convert_fusion.9
  1032.0 41.3 %reduce-scatter.15.cloned.1.call-done = bf16[256,1024]{1,0:T(8,128)(2,1)} async-done(((bf16[1024,1024]{1,0:T(8,128)(2,1)}), bf16[256,1024]{1,0:T(8,128)(2,1)}) %reduce-scatter.15.cloned.1.call-update) | async-done | bytes 524304 | tf_op jit(solution)/shard_map/reduce_scatter | solution.py:150
  1076.2 17.4 %collective-permute-done.5 = bf16[256,1024]{1,0:T(8,128)(2,1)S(1)} collective-permute-done((bf16[256,1024]{1,0:T(8,128)(2,1)S(1)}, bf16[256,1024]{1,0:T(8,128)(2,1)S(1)}, u32[]{:S(2)}, u32[]{:S(2)}) %collective-permute-start.5) | collective-permute-done | bytes 524320 | tf_op jit(solution)/shard_map/ppermute | solution.py:156
  1095.5 6.2 bitcast_convert_fusion
  1101.9 23.1 %psum.78 = f32[2,1536]{1,0:T(2,128)S(1)} all-reduce(f32[2,1536]{1,0:T(2,128)S(1)} %pad_maximum_fusion.1), channel_id=1, replica_groups=mesh['section'=2,'tensor'=4,'dp'=4] {'section','dp'}, use_global_device_ids=true, to_apply=%region_50.51 | all-reduce | flops 3072 | bytes 24576 | tf_op jit(solution)/shard_map/psum | solution.py:315
  1126.3 14.4 %all-reduce.9.cloned.1.call-done = (bf16[1024,768]{1,0:T(8,128)(2,1)}, bf16[256,1024]{1,0:T(8,128)(2,1)}) async-done(((bf16[1024,768]{1,0:T(8,128)(2,1)}, bf16[256,1024]{1,0:T(8,128)(2,1)}), (bf16[1024,768]{1,0:T(8,128)(2,1)}, bf16[256,1024]{1,0:T(8,128)(2,1)})) %all-reduce.9.cloned.1.call-update) | async-done | bytes 2097168 | tf_op jit(solution)/shard_map/psum | solution.py:233
  1144.0 3.5 copy.34
  1147.5 3.8 copy.35
  1153.6 32.4 %reduce-scatter.23.cloned.1.call-done = bf16[256,1024]{1,0:T(8,128)(2,1)} async-done(((bf16[1024,1024]{1,0:T(8,128)(2,1)}), bf16[256,1024]{1,0:T(8,128)(2,1)}) %reduce-scatter.23.cloned.1.call-update) | async-done | bytes 524304 | tf_op jit(solution)/shard_map/reduce_scatter | solution.py:150
  1192.5 45.0 %psum.70 = f32[2,6,1024]{2,1,0:T(8,128)S(1)} all-reduce(f32[2,6,1024]{2,1,0:T(8,128)S(1)} %pad_maximum_fusion), channel_id=1, replica_groups=mesh['section'=2,'tensor'=4,'dp'=4] {'section','dp','tensor'}, use_global_device_ids=true, to_apply=%region_36.37 | all-reduce | flops 12288 | bytes 98304 | tf_op jit(solution)/shard_map/psum | solution.py:316
  (282 shorter events, 108.5 us)
Async XLA Ops:
  7.2 61.2 %all-gather.10.cloned.1.call-start = ((), (), s32[]{:S(2)}) async-start(), calls=%async_computation.8 | async-start | bytes 2621440 | tf_op jit(solution)/shard_map/all_gather | solution.py:146
  13.7 6.1 collective-permute-start
  22.0 104.8 %reduce-scatter.9.cloned.1.call-start = ((), (), s32[]{:S(2)}) async-start(), calls=%async_computation.9 | async-start | bytes 2621440 | tf_op jit(solution)/shard_map/reduce_scatter | solution.py:150
  25.4 37.5 %collective-permute-start.1 = (bf16[1024,768]{1,0:T(8,128)(2,1)}, bf16[1024,768]{1,0:T(8,128)(2,1)S(1)}, u32[]{:S(2)}, u32[]{:S(2)}) collective-permute-start(bf16[1024,768]{1,0:T(8,128)(2,1)} %copy.32), channel_id=1, source_target_pairs={{0,16},{16,0},{1,17},{17,1},{2,18},{18,2},{3,19},{19,3},{4,20},{20... | collective-permute-start | bytes 4718600 | tf_op jit(solution)/shard_map/ppermute | solution.py:156
  26.0 56.3 %collective-permute-start.2 = (bf16[256,1024]{1,0:T(8,128)(2,1)S(1)}, bf16[256,1024]{1,0:T(8,128)(2,1)S(1)}, u32[]{:S(2)}, u32[]{:S(2)}) collective-permute-start(bf16[256,1024]{1,0:T(8,128)(2,1)S(1)} %bitcast.205), channel_id=1, source_target_pairs={{0,16},{16,0},{1,17},{17,1},{2,18},{18,2},{3,19},{19,3},{4,20},{20... | collective-permute-start | bytes 1572872 | tf_op jit(solution)/shard_map/ppermute | solution.py:156
  82.4 44.4 %copy-start.8 = (bf16[2,256,1024]{2,1,0:T(8,128)(2,1)S(1)}, bf16[2,256,1024]{2,1,0:T(8,128)(2,1)}, u32[]{:S(2)}) copy-start(bf16[2,256,1024]{2,1,0:T(8,128)(2,1)} %param.14) | copy-start | bytes 3145732
  84.5 95.6 %all-gather.12.cloned.1.call-start = ((), (), s32[]{:S(2)}) async-start(), calls=%async_computation.10 | async-start | bytes 2621440 | tf_op jit(solution)/shard_map/all_gather | solution.py:146
  130.7 142.5 %reduce-scatter.11.cloned.1.call-start = ((), (), s32[]{:S(2)}) async-start(), calls=%async_computation.11 | async-start | bytes 2621440 | tf_op jit(solution)/shard_map/reduce_scatter | solution.py:150
  131.2 48.9 %collective-permute-start.3 = (bf16[1024,1024]{1,0:T(8,128)(2,1)}, bf16[1024,1024]{1,0:T(8,128)(2,1)}, u32[]{:S(2)}, u32[]{:S(2)}) collective-permute-start(bf16[1024,1024]{1,0:T(8,128)(2,1)} %bitcast.220), channel_id=1, source_target_pairs={{0,16},{16,0},{1,17},{17,1},{2,18},{18,2},{3,19},{19,3},{4,20},{20... | collective-permute-start | bytes 6291464 | tf_op jit(solution)/shard_map/ppermute | solution.py:156
  132.7 91.0 %collective-permute-start.4 = (bf16[1024,1024]{1,0:T(8,128)(2,1)}, bf16[1024,1024]{1,0:T(8,128)(2,1)}, u32[]{:S(2)}, u32[]{:S(2)}) collective-permute-start(bf16[1024,1024]{1,0:T(8,128)(2,1)} %bitcast.221), channel_id=1, source_target_pairs={{0,16},{16,0},{1,17},{17,1},{2,18},{18,2},{3,19},{19,3},{4,20},{20... | collective-permute-start | bytes 6291464 | tf_op jit(solution)/shard_map/ppermute | solution.py:156
  180.1 43.6 %copy-start.51 = (bf16[1,1024,1024]{2,1,0:T(8,128)(2,1)S(1)}, bf16[1,1024,1024]{2,1,0:T(8,128)(2,1)}, u32[]{:S(2)}) copy-start(bf16[1,1024,1024]{2,1,0:T(8,128)(2,1)} %param.26) | copy-start | bytes 6291460
  184.8 38.9 %copy-start.57 = (f32[1024,1024]{1,0:T(8,128)}, f32[1024,1024]{1,0:T(8,128)S(1)}, u32[]{:S(2)}) copy-start(f32[1024,1024]{1,0:T(8,128)S(1)} %fusion.62) | copy-start | bytes 12582916
  228.0 93.4 %all-gather.14.cloned.1.call-start = ((), (), s32[]{:S(2)}) async-start(), calls=%async_computation.12 | async-start | bytes 2621440 | tf_op jit(solution)/shard_map/all_gather | solution.py:146
  274.6 46.8 %copy-start.35 = (bf16[1024,768]{1,0:T(8,128)(2,1)S(1)}, bf16[1024,768]{1,0:T(8,128)(2,1)}, u32[]{:S(2)}) copy-start(bf16[1024,768]{1,0:T(8,128)(2,1)} %copy.32) | copy-start | bytes 4718596
  276.0 103.8 %reduce-scatter.13.cloned.1.call-start = ((), (), s32[]{:S(2)}) async-start(), calls=%async_computation.13 | async-start | bytes 2621440 | tf_op jit(solution)/shard_map/reduce_scatter | solution.py:150
  325.2 10.1 copy-start.32
  337.4 91.6 %all-gather.16.cloned.1.call-start = ((), (), s32[]{:S(2)}) async-start(), calls=%async_computation.14 | async-start | bytes 2621440 | tf_op jit(solution)/shard_map/all_gather | solution.py:146
  383.6 91.7 %all-gather.24.cloned.1.call-start = ((), (), s32[]{:S(2)}) async-start(), calls=%async_computation.23 | async-start | bytes 2621440 | tf_op jit(solution)/shard_map/all_gather | solution.py:146
  385.8 146.9 %reduce-scatter.17.cloned.1.call-start = ((), (), s32[]{:S(2)}) async-start(), calls=%async_computation.16 | async-start | bytes 2621440 | tf_op jit(solution)/shard_map/reduce_scatter | solution.py:150
  475.4 10.3 copy-start.49
  490.9 45.1 %copy-start.24 = (bf16[1,256,1024]{2,1,0:T(8,128)(2,1)S(1)}, bf16[1,256,1024]{2,1,0:T(8,128)(2,1)}, u32[]{:S(2)}) copy-start(bf16[1,256,1024]{2,1,0:T(8,128)(2,1)} %get-tuple-element.105) | copy-start | bytes 1572868
  491.0 92.9 %all-gather.18.cloned.1.call-start = ((), (), s32[]{:S(2)}) async-start(), calls=%async_computation.17 | async-start | bytes 2621440 | tf_op jit(solution)/shard_map/all_gather | solution.py:146
  536.6 47.3 %copy-start.29 = (bf16[1,256,1024]{2,1,0:T(8,128)(2,1)S(1)}, bf16[1,256,1024]{2,1,0:T(8,128)(2,1)}, u32[]{:S(2)}) copy-start(bf16[1,256,1024]{2,1,0:T(8,128)(2,1)} %param.20) | copy-start | bytes 1572868
  536.7 47.3 %copy-start.33 = (bf16[256,1024]{1,0:T(8,128)(2,1)S(1)}, bf16[256,1024]{1,0:T(8,128)(2,1)}, u32[]{:S(2)}) copy-start(bf16[256,1024]{1,0:T(8,128)(2,1)} %copy-done.31) | copy-start | bytes 1572868
  538.5 112.1 %reduce-scatter.19.cloned.1.call-start = ((), (), s32[]{:S(2)}) async-start(), calls=%async_computation.18 | async-start | bytes 2621440 | tf_op jit(solution)/shard_map/reduce_scatter | solution.py:150
  607.9 92.7 %all-gather.20.cloned.1.call-start = ((), (), s32[]{:S(2)}) async-start(), calls=%async_computation.19 | async-start | bytes 2621440 | tf_op jit(solution)/shard_map/all_gather | solution.py:146
  655.1 129.1 %all-reduce.15.cloned.1.call-start = ((), (), s32[]{:S(2)}) async-start(), calls=%async_computation.27 | async-start | bytes 8388608 | tf_op jit(solution)/shard_map/psum | solution.py:233
  665.7 165.2 %reduce-scatter.21.cloned.1.call-start = ((), (), s32[]{:S(2)}) async-start(), calls=%async_computation.20 | async-start | bytes 2621440 | tf_op jit(solution)/shard_map/reduce_scatter | solution.py:150
  713.9 181.3 %all-reduce.13.cloned.1.call-start = ((), (), s32[]{:S(2)}) async-start(), calls=%async_computation.26 | async-start | bytes 4194304 | tf_op jit(solution)/shard_map/psum | solution.py:233
  722.2 108.7 %copy-start.9 = (bf16[2,256,1024]{2,1,0:T(8,128)(2,1)S(1)}, bf16[2,256,1024]{2,1,0:T(8,128)(2,1)}, u32[]{:S(2)}) copy-start(bf16[2,256,1024]{2,1,0:T(8,128)(2,1)} %param.14) | copy-start | bytes 3145732
  784.2 158.3 %all-gather.22.cloned.1.call-start = ((), (), s32[]{:S(2)}) async-start(), calls=%async_computation.21 | async-start | bytes 2621440 | tf_op jit(solution)/shard_map/all_gather | solution.py:146
  837.1 189.5 %all-reduce.11.cloned.1.call-start = ((), (), s32[]{:S(2)}) async-start(), calls=%async_computation.25 | async-start | bytes 8388608 | tf_op jit(solution)/shard_map/psum | solution.py:233
  895.3 178.0 %reduce-scatter.15.cloned.1.call-start = ((), (), s32[]{:S(2)}) async-start(), calls=%async_computation.15 | async-start | bytes 2621440 | tf_op jit(solution)/shard_map/reduce_scatter | solution.py:150
  903.0 39.5 %copy-start.30 = (bf16[1,256,1024]{2,1,0:T(8,128)(2,1)S(1)}, bf16[1,256,1024]{2,1,0:T(8,128)(2,1)}, u32[]{:S(2)}) copy-start(bf16[1,256,1024]{2,1,0:T(8,128)(2,1)} %param.20) | copy-start | bytes 1572868
  903.0 39.5 %copy-start.34 = (bf16[256,1024]{1,0:T(8,128)(2,1)S(1)}, bf16[256,1024]{1,0:T(8,128)(2,1)}, u32[]{:S(2)}) copy-start(bf16[256,1024]{1,0:T(8,128)(2,1)} %copy-done.31) | copy-start | bytes 1572868
  903.0 237.7 %all-reduce.9.cloned.1.call-start = ((), (), s32[]{:S(2)}) async-start(), calls=%async_computation.24 | async-start | bytes 4194304 | tf_op jit(solution)/shard_map/psum | solution.py:233
  1026.6 159.5 %reduce-scatter.23.cloned.1.call-start = ((), (), s32[]{:S(2)}) async-start(), calls=%async_computation.22 | async-start | bytes 2621440 | tf_op jit(solution)/shard_map/reduce_scatter | solution.py:150
  1032.0 41.3 %copy-start.12 = (bf16[256,1024]{1,0:T(8,128)(2,1)S(1)}, bf16[256,1024]{1,0:T(8,128)(2,1)}, u32[]{:S(2)}) copy-start(bf16[256,1024]{1,0:T(8,128)(2,1)} %reduce-scatter.13.cloned.1.call-done) | copy-start | bytes 1572868
  1073.3 20.4 %copy-start.27 = (bf16[256,1024]{1,0:T(8,128)(2,1)S(1)}, bf16[256,1024]{1,0:T(8,128)(2,1)}, u32[]{:S(2)}) copy-start(bf16[256,1024]{1,0:T(8,128)(2,1)} %reduce-scatter.15.cloned.1.call-done) | copy-start | bytes 1572868
  1074.7 18.9 %collective-permute-start.5 = (bf16[256,1024]{1,0:T(8,128)(2,1)S(1)}, bf16[256,1024]{1,0:T(8,128)(2,1)S(1)}, u32[]{:S(2)}, u32[]{:S(2)}) collective-permute-start(bf16[256,1024]{1,0:T(8,128)(2,1)S(1)} %broadcast_select_fusion.23), channel_id=1, source_target_pairs={{0,16},{16,0},{1,17},{17,1},{2,18},{18,2},{3,19},{19,3},{4,20},{20... | collective-permute-start | bytes 1572872 | tf_op jit(solution)/shard_map/ppermute | solution.py:156
  1151.3 34.7 %copy-start.10 = (bf16[2,256,1024]{2,1,0:T(8,128)(2,1)S(1)}, bf16[2,256,1024]{2,1,0:T(8,128)(2,1)}, u32[]{:S(2)}) copy-start(bf16[2,256,1024]{2,1,0:T(8,128)(2,1)} %param.14) | copy-start | bytes 3145732
  1151.3 34.7 %copy-start.42 = (f32[1024]{0:T(1024)S(1)}, f32[1024]{0:T(1024)}, u32[]{:S(2)}) copy-start(f32[1024]{0:T(1024)} %copy-done.41) | copy-start | bytes 12292
  1151.3 34.7 %copy-start.44 = (f32[256]{0:T(256)S(1)}, f32[256]{0:T(256)}, u32[]{:S(2)}) copy-start(f32[256]{0:T(256)} %copy-done.43) | copy-start | bytes 3076
  1151.3 36.2 %copy-start.48 = (f32[256]{0:T(256)S(1)}, f32[256]{0:T(256)}, u32[]{:S(2)}) copy-start(f32[256]{0:T(256)} %copy-done.47) | copy-start | bytes 3076
  1151.3 36.3 %copy-start.46 = (f32[256]{0:T(256)S(1)}, f32[256]{0:T(256)}, u32[]{:S(2)}) copy-start(f32[256]{0:T(256)} %copy-done.45) | copy-start | bytes 3076
  1151.4 37.9 %copy-start.16 = (bf16[256,1024]{1,0:T(8,128)(2,1)S(1)}, bf16[256,1024]{1,0:T(8,128)(2,1)}, u32[]{:S(2)}) copy-start(bf16[256,1024]{1,0:T(8,128)(2,1)} %get-tuple-element.101) | copy-start | bytes 1572868
  1151.4 37.9 %copy-start.20 = (f32[256,1024]{1,0:T(8,128)S(1)}, f32[256,1024]{1,0:T(8,128)}, u32[]{:S(2)}) copy-start(f32[256,1024]{1,0:T(8,128)} %copy-done.19) | copy-start | bytes 3145732
  1191.0 47.2 %collective-permute-start.6 = (bf16[256,1024]{1,0:T(8,128)(2,1)}, bf16[256,1024]{1,0:T(8,128)(2,1)S(1)}, u32[]{:S(2)}, u32[]{:S(2)}) collective-permute-start(bf16[256,1024]{1,0:T(8,128)(2,1)} %get-tuple-element.108), channel_id=1, source_target_pairs={{0,16},{16,0},{1,17},{17,1},{2,18},{18,2},{3,19},{19,3},{4,20},{20... | collective-permute-start | bytes 1572872 | tf_op jit(solution)/shard_map/ppermute | solution.py:156
  (41 other events, 142.0 us)
Sparse Core Ops, SparseCore 0:
  22.1 46.2 all-gather.9
  84.6 42.1 reduce-scatter.8
  130.8 45.2 all-gather.11
  228.1 45.0 reduce-scatter.10
  276.1 45.2 all-gather.13
  337.5 42.1 reduce-scatter.12
  383.7 45.2 all-gather.15
  430.7 44.6 all-gather.23
  491.1 41.6 reduce-scatter.16
  538.6 45.2 all-gather.17
  608.0 42.5 reduce-scatter.18
  655.3 45.2 all-gather.19
  704.2 79.9 all-reduce.14
  786.9 43.9 reduce-scatter.20
  834.4 60.8 all-reduce.12
  897.3 45.1 all-gather.21
  946.6 79.9 all-reduce.10
  1029.3 43.9 reduce-scatter.14
  1077.5 63.1 all-reduce.8
  1142.9 43.0 reduce-scatter.22

commit v2 on v1

--- a/solution.py
+++ b/solution.py
@@ -152,8 +152,60 @@
     ).astype(jnp.float32)
 
 
+def gathered_early(block):
+    size, place = lax.axis_size("tensor"), lax.axis_index("tensor")
+    rows = block.shape[0]
+    whole = jnp.zeros((size * rows, block.shape[1]), block.dtype)
+    for step in range(size):
+        route = [(i, (i + step) % size) for i in range(size)]
+        piece = lax.ppermute(block, "tensor", route) if step else block
+        origin = lax.rem(place - step + size, size)
+        whole = lax.dynamic_update_slice_in_dim(whole, piece, origin * rows, 0)
+    return whole
+
+
+def partner(block, distance):
+    return lax.ppermute(block, "dp", [(i, i ^ distance) for i in range(lax.axis_size("dp"))])
+
+
+def joined(block, other, bit):
+    lower = jnp.where(bit == 0, block, other)
+    upper = jnp.where(bit == 0, other, block)
+    return jnp.concatenate([lower, upper], axis=0)
+
+
+def half_of(block, which):
+    rows = block.shape[0] // 2
+    return lax.dynamic_slice_in_dim(block, which * rows, rows, 0)
+
+
 def swapped(block):
     return lax.ppermute(block, "section", [(0, 1), (1, 0)])
+
+
+def fetched(block):
+    core = lax.rem(lax.axis_index("dp"), 2)
+    got = swapped(half_of(block, core))
+    return joined(got, partner(got, 1), core)
+
+
+def total(block, owner):
+    place = lax.axis_index("dp")
+    distances = []
+    while 2 ** len(distances) < lax.axis_size("dp"):
+        distances.append(2 ** len(distances))
+    for distance in distances:
+        bit = lax.rem(place // distance, 2)
+        got = partner(half_of(block, 1 - bit), distance)
+        block = (half_of(block, bit).astype(jnp.float32) + got.astype(jnp.float32)).astype(
+            block.dtype
+        )
+    got = lax.ppermute(block, "section", [(1 - owner, owner)])
+    block = (block.astype(jnp.float32) + got.astype(jnp.float32)).astype(block.dtype)
+    for distance in reversed(distances):
+        bit = lax.rem(place // distance, 2)
+        block = joined(block, partner(block, distance), bit)
+    return block
 
 
 def layer_forward(layer_input, weights):
@@ -164,7 +216,9 @@
     normed = gathered(layer_norm(residual, gain_one, shift_one).astype(jnp.bfloat16))
     projected = (dot(normed, attend) + attend_offset).astype(jnp.bfloat16)
     blended, logsum = attend_forward(projected)
-    middle = residual + scattered(dot(blended, mixing)) + mixing_offset
+    mixed = scattered(dot(blended, mixing))
+    mixed, expand, shrink = lax.optimization_barrier((mixed, expand, shrink))
+    middle = residual + mixed + mixing_offset
     feed = gathered(layer_norm(middle, gain_two, shift_two).astype(jnp.bfloat16))
     hidden_pre = dot(feed, expand) + expand_offset
     hidden = smooth_gate(hidden_pre).astype(jnp.bfloat16)
@@ -173,13 +227,12 @@
     return result, (layer_input, normed, projected, logsum, blended, middle, feed, hidden_pre)
 
 
-def layer_backward(out_change, weights, kept):
+def layer_backward(out_change, change_full, weights, kept):
     attend, mixing, expand, shrink, rows = weights
     gain_one, shift_one, mixing_offset, gain_two, shift_two, shrink_offset = rows[:6]
     layer_input, normed, projected, logsum, blended, middle, feed, hidden_pre = kept
     gate_value, gate_back = jax.vjp(smooth_gate, hidden_pre)
     hidden = gate_value.astype(jnp.bfloat16)
-    change_full = gathered(out_change)
     shrink_change = dot(change_full, hidden, contract_rows).astype(jnp.bfloat16)
     pre_change = gate_back(dot(change_full, shrink))[0].astype(jnp.bfloat16)
     expand_change = dot(feed, pre_change, contract_rows).astype(jnp.bfloat16)
@@ -220,18 +273,11 @@
     column_changes = jnp.concatenate([bias_change, expand_row_change])
     return (
         input_change,
-        (expand_change, shrink_change),
-        (attend_change, mixing_change),
+        jnp.concatenate([expand_change, shrink_change], axis=0),
+        jnp.concatenate([attend_change.reshape(-1, mixing.shape[1]), mixing_change], axis=0),
         row_changes,
         column_changes,
     )
-
-
-def total(blocks, after=None):
-    if after is not None:
-        blocks, after = lax.optimization_barrier((blocks, after))
-    sums = lax.psum(blocks, ("section", "dp"))
-    return sums, after
 
 
 def body(
@@ -252,7 +298,6 @@
 ):
     micro_count, local_rows, model_width = block_input.shape
     local_width = attend_weight.shape[3]
-    hidden_width = expand_weight.shape[2]
     section_index = lax.axis_index("section")
     early = section_index == 0
 
@@ -276,7 +321,7 @@
         shrink_weight[0],
         small,
     )
-    other = jax.tree.map(swapped, own)
+    other = tuple(fetched(block) for block in own[:4]) + (swapped(small),)
 
     def weights_of(layer):
         attend, mixing, expand, shrink, row = (
@@ -297,33 +342,45 @@
 
     first_result, first_kept = layer_forward(taken, weights[0])
     second_result, second_kept = layer_forward(first_result, weights[1])
-    second_back = layer_backward(given, weights[1], second_kept)
-    first_back = layer_backward(second_back[0], weights[0], first_kept)
+    second_back = layer_backward(given, gathered_early(given), weights[1], second_kept)
+    first_back = layer_backward(
+        second_back[0], gathered(second_back[0]), weights[0], first_kept
+    )
 
     def placed(first, second):
-        mine = jnp.where(early, first, second)
-        theirs = swapped(jnp.where(early, second, first))
-        return jnp.stack([jnp.where(early, mine, theirs), jnp.where(early, theirs, mine)])[None]
+        earlier = lax.ppermute(first, "section", [(1, 0)])
+        later = lax.ppermute(second, "section", [(0, 1)])
+        return jnp.where(early, jnp.stack([first, earlier]), jnp.stack([later, second]))[None]
 
     section_output = placed(first_result, second_result)
     input_changes = placed(first_back[0], second_back[0])
 
-    late_wide, mark = total(second_back[1])
-    late_narrow, mark = total(second_back[2], late_wide)
-    soon_wide, mark = total(first_back[1], late_narrow)
-    soon_narrow, mark = total(first_back[2], soon_wide)
-    columns = lax.psum(jnp.stack([first_back[4], second_back[4]]), ("section", "dp"))
-    rows = lax.psum(
-        jnp.stack([first_back[3], second_back[3]]), ("section", "dp", "tensor")
-    )
+    wide = [total(first_back[1], 0), total(second_back[1], 1)]
+    narrow = [total(first_back[2], 0), total(second_back[2], 1)]
+
+    shards, shard = lax.axis_size("tensor"), lax.axis_index("tensor")
+    row_changes = jnp.stack([first_back[3], second_back[3]])
+    column_changes = jnp.stack([first_back[4], second_back[4]])
+    spread = jnp.where(
+        (jnp.arange(shards) == shard)[:, None], column_changes.reshape(1, -1), 0.0
+    )
+    sums = lax.psum(
+        jnp.concatenate([row_changes.reshape(-1), spread.reshape(-1)]),
+        ("section", "dp", "tensor"),
+    )
+    rows = sums[: row_changes.size].reshape(row_changes.shape)
+    columns = lax.dynamic_index_in_dim(
+        sums[row_changes.size :].reshape(spread.shape), shard, 0, keepdims=False
+    ).reshape(column_changes.shape)
 
     def chosen(first, second):
         return jnp.where(early, first, second).astype(jnp.float32)
 
-    expand_total = chosen(soon_wide[0], late_wide[0])
-    shrink_total = chosen(soon_wide[1], late_wide[1])
-    attend_total = chosen(soon_narrow[0], late_narrow[0])
-    mixing_total = chosen(soon_narrow[1], late_narrow[1])
+    wide_total = chosen(*wide)
+    narrow_total = chosen(*narrow)
+    expand_total, shrink_total = wide_total[:model_width], wide_total[model_width:]
+    attend_rows = 3 * local_width
+    attend_total, mixing_total = narrow_total[:attend_rows], narrow_total[attend_rows:]
     column_total = chosen(columns[0], columns[1])
     row_total = chosen(rows[0], rows[1])
     return (

time: 1260 us -> 1120 us (0.89)
  waiting for transfers between devices: 909 us -> 732 us
  blocking collectives: 68.1 us -> 0 us
  other arithmetic: 58.6 us -> 112 us
  local copies, waits for them, and re-layouts: 30.6 us -> 70.6 us
  starting transfers between devices: 12.8 us -> 45.7 us
  matrix products: 108 us -> 88.1 us
    ppermute x0 -> x31, waiting for transfers between devices: none -> 153 us  [the longest x20 78.2 us: partner(): lax.ppermute(block, 'dp', [(i, i ^ distance) for i in range(lax.axis_size...]
    reduce_scatter x8, waiting for transfers between devices: 334 us -> 216 us  [scattered(): lax.psum_scatter(block.astype(jnp.bfloat16), 'tensor', scatter_dimension=...]
    psum x4 -> x1, waiting for transfers between devices: 184 us -> 101 us  [body(): lax.psum(jnp.concatenate([row_changes.reshape(-1), spread.reshape(-1)]),...]
    ppermute x7 -> x5, waiting for transfers between devices: 139 us -> 67.7 us  [swapped(): return lax.ppermute(block, 'section', [(0, 1), (1, 0)])]
    psum x2 -> x0, blocking collectives: 68.1 us -> none  [the longest x1 45 us: body(): lax.psum(jnp.stack([first_back[3], second_back[3]]), ('section', 'dp', 't...]
    all_gather x8 -> x7, waiting for transfers between devices: 252 us -> 195 us  [gathered(): return lax.all_gather(block, 'tensor', axis=0, tiled=True)]
    ppermute x0 -> x31, starting transfers between devices: none -> 36.3 us  [the longest x20 11.3 us: partner(): lax.ppermute(block, 'dp', [(i, i ^ distance) for i in range(lax.axis_size...]
    convert_element_type x0 -> x16, other arithmetic: none -> 28.9 us  [the longest x8 16.8 us: total(): (half_of(block, bit).astype(jnp.float32) + got.astype(jnp.float32)).astyp...]
  transfers between devices with their start and end apart: 27 -> 52, of which waited for: 23 -> 30; matrix products, arithmetic and copies ran while one was open for 9% -> 16% of each run, Pallas kernels for 2% -> 1%
where the time goes in v2:
time: 1120 us; the launch traced here: 1110 us
  waiting for transfers between devices  732 us (65%)
  other arithmetic  112 us (10%)
  matrix products  88.1 us (8%)
  local copies, waits for them, and re-layouts  70.6 us (6%)
  starting transfers between devices  45.7 us (4%)
  Pallas kernels  45.3 us (4%)
  between operations  15.9 us (1%)
    reduce_scatter x8, waiting for transfers between devices, scattered(): lax.psum_scatter(block.astype(jnp.bfloat16), 'tensor', scatter_dimension=...  216 us
    all_gather x7, waiting for transfers between devices, gathered(): return lax.all_gather(block, 'tensor', axis=0, tiled=True)  195 us
    psum x1, waiting for transfers between devices, body(): lax.psum(jnp.concatenate([row_changes.reshape(-1), spread.reshape(-1)]),...  101 us
    dot_general x24, matrix products, dot(): lax.dot_general(left, right, dims, preferred_element_type=jnp.float32)  88.1 us
    ppermute x20, waiting for transfers between devices, partner(): lax.ppermute(block, 'dp', [(i, i ^ distance) for i in range(lax.axis_size...  78.2 us
    ppermute x5, waiting for transfers between devices, swapped(): return lax.ppermute(block, 'section', [(0, 1), (1, 0)])  67.7 us
    ppermute x3, waiting for transfers between devices, gathered_early(): piece = lax.ppermute(block, 'tensor', route) if step else block  56.1 us
    unnamed x227, local copies, waits for them, and re-layouts  32.7 us
  transfers between devices with their start and end apart: 52, of which 30 were waited for; matrix products, arithmetic and copies ran while one was open for 16% of the time, Pallas kernels for 1%

profile of v2, /device:TPU:0, one launch (start us, length us, event | category | flops | bytes accessed | tf_op | source)
XLA Modules:
  0.0 1110.1 jit_solution(12437248272751528678)
XLA Ops:
  26.1 18.5 %collective-permute-done.1 = bf16[512,768]{0,1:T(8,128)(2,1)} collective-permute-done((bf16[512,768]{0,1:T(8,128)(2,1)S(1)}, bf16[512,768]{0,1:T(8,128)(2,1)}, u32[]{:S(2)}, u32[]{:S(2)}) %collective-permute-start.1) | collective-permute-done | bytes 786464 | tf_op jit(solution)/shard_map/ppermute | solution.py:183
  44.5 4.0 collective-permute-done.3
  54.3 14.2 %all-gather.8.cloned.1.call-done = bf16[1024,1024]{1,0:T(8,128)(2,1)} async-done(((bf16[256,1024]{1,0:T(8,128)(2,1)}), bf16[1024,1024]{1,0:T(8,128)(2,1)}) %all-gather.8.cloned.1.call-update) | async-done | bytes 2097168 | tf_op jit(solution)/shard_map/all_gather | solution.py:146
  72.3 9.1 attend_forward.2
  89.3 23.9 %collective-permute-done.5 = bf16[512,1024]{1,0:T(8,128)(2,1)S(1)} collective-permute-done((bf16[512,1024]{1,0:T(8,128)(2,1)S(1)}, bf16[512,1024]{1,0:T(8,128)(2,1)S(1)}, u32[]{:S(2)}, u32[]{:S(2)}) %collective-permute-start.5) | collective-permute-done | bytes 1048608 | tf_op jit(solution)/shard_map/ppermute | solution.py:183
  113.2 21.3 %collective-permute-done.7 = bf16[512,1024]{1,0:T(8,128)(2,1)S(1)} collective-permute-done((bf16[512,1024]{1,0:T(8,128)(2,1)S(1)}, bf16[512,1024]{1,0:T(8,128)(2,1)S(1)}, u32[]{:S(2)}, u32[]{:S(2)}) %collective-permute-start.7) | collective-permute-done | bytes 1048608 | tf_op jit(solution)/shard_map/ppermute | solution.py:183
  147.7 45.0 %all-gather.10.cloned.1.call-done = bf16[1024,1024]{1,0:T(8,128)(2,1)} async-done(((bf16[256,1024]{1,0:T(8,128)(2,1)}), bf16[1024,1024]{1,0:T(8,128)(2,1)}) %all-gather.10.cloned.1.call-update) | async-done | bytes 2097168 | tf_op jit(solution)/shard_map/all_gather | solution.py:146
  192.7 4.7 fusion.91
  199.4 4.1 convolution_convert_fusion.8
  203.6 42.7 %reduce-scatter.11.cloned.1.call-done = bf16[256,1024]{1,0:T(8,128)(2,1)} async-done(((bf16[1024,1024]{1,0:T(8,128)(2,1)}), bf16[256,1024]{1,0:T(8,128)(2,1)}) %reduce-scatter.11.cloned.1.call-update) | async-done | bytes 524304 | tf_op jit(solution)/shard_map/reduce_scatter | solution.py:150
  249.6 44.8 %all-gather.12.cloned.1.call-done = bf16[1024,1024]{1,0:T(8,128)(2,1)} async-done(((bf16[256,1024]{1,0:T(8,128)(2,1)}), bf16[1024,1024]{1,0:T(8,128)(2,1)}) %all-gather.12.cloned.1.call-update) | async-done | bytes 2097168 | tf_op jit(solution)/shard_map/all_gather | solution.py:146
  298.0 9.1 attend_forward.3
  310.3 43.2 %reduce-scatter.13.cloned.1.call-done = bf16[256,1024]{1,0:T(8,128)(2,1)} async-done(((bf16[1024,1024]{1,0:T(8,128)(2,1)}), bf16[256,1024]{1,0:T(8,128)(2,1)}) %reduce-scatter.13.cloned.1.call-update) | async-done | bytes 524304 | tf_op jit(solution)/shard_map/reduce_scatter | solution.py:150
  363.2 18.4 %collective-permute-done.11 = bf16[256,1024]{1,0:T(8,128)(2,1)} collective-permute-done((bf16[256,1024]{1,0:T(8,128)(2,1)S(1)}, bf16[256,1024]{1,0:T(8,128)(2,1)}, u32[]{:S(2)}, u32[]{:S(2)}) %collective-permute-start.11) | collective-permute-done | bytes 524320 | tf_op jit(solution)/shard_map/ppermute | solution.py:161
  383.5 37.6 %collective-permute-done.12 = bf16[256,1024]{1,0:T(8,128)(2,1)} collective-permute-done((bf16[256,1024]{1,0:T(8,128)(2,1)S(1)}, bf16[256,1024]{1,0:T(8,128)(2,1)}, u32[]{:S(2)}, u32[]{:S(2)}) %collective-permute-start.12) | collective-permute-done | bytes 524320 | tf_op jit(solution)/shard_map/ppermute | solution.py:161
  423.8 12.2 %all-gather.14.cloned.1.call-done = bf16[1024,1024]{1,0:T(8,128)(2,1)} async-done(((bf16[256,1024]{1,0:T(8,128)(2,1)}), bf16[1024,1024]{1,0:T(8,128)(2,1)}) %all-gather.14.cloned.1.call-update) | async-done | bytes 2097168 | tf_op jit(solution)/shard_map/all_gather | solution.py:146
  436.0 4.7 fusion.92
  440.8 5.1 convert_reduce_fusion
  450.9 7.0 convolution_convert_fusion.6
  458.0 43.4 %reduce-scatter.17.cloned.1.call-done = bf16[256,1024]{1,0:T(8,128)(2,1)} async-done(((bf16[1024,1024]{1,0:T(8,128)(2,1)}), bf16[256,1024]{1,0:T(8,128)(2,1)}) %reduce-scatter.17.cloned.1.call-update) | async-done | bytes 524304 | tf_op jit(solution)/shard_map/reduce_scatter | solution.py:150
  502.9 44.1 %reduce-scatter.15.cloned.1.call-done = bf16[256,1024]{1,0:T(8,128)(2,1)} async-done(((bf16[1024,1024]{1,0:T(8,128)(2,1)}), bf16[256,1024]{1,0:T(8,128)(2,1)}) %reduce-scatter.15.cloned.1.call-update) | async-done | bytes 524304 | tf_op jit(solution)/shard_map/reduce_scatter | solution.py:150
  551.7 45.2 %all-gather.16.cloned.1.call-done = bf16[1024,1024]{1,0:T(8,128)(2,1)} async-done(((bf16[256,1024]{1,0:T(8,128)(2,1)}), bf16[1024,1024]{1,0:T(8,128)(2,1)}) %all-gather.16.cloned.1.call-update) | async-done | bytes 2097168 | tf_op jit(solution)/shard_map/all_gather | solution.py:146
  600.6 13.3 %attend_backward.2 = (bf16[1024,256]{1,0:T(8,128)(2,1)S(1)}, bf16[1024,256]{1,0:T(8,128)(2,1)S(1)}, bf16[1024,256]{1,0:T(8,128)(2,1)S(1)}) custom-call(bf16[1024,768]{1,0:T(8,128)(2,1)S(1)} %copy-done.3, bf16[1024,768]{1,0:T(8,128)(2,1)S(1)} %copy-done.3, bf16[1024,768]{1,0:T(8,128)(2,1)S(1)} %copy-done.3, ...), custom_call_target="tpu_custom_call" | custom-call | flops 2684354560 | bytes 4718592 | tf_op jit(solution)/shard_map/attend_backward/pallas_call | solution.py:127
  619.6 42.7 %reduce-scatter.19.cloned.1.call-done = bf16[256,1024]{1,0:T(8,128)(2,1)} async-done(((bf16[1024,1024]{1,0:T(8,128)(2,1)}), bf16[256,1024]{1,0:T(8,128)(2,1)}) %reduce-scatter.19.cloned.1.call-update) | async-done | bytes 524304 | tf_op jit(solution)/shard_map/reduce_scatter | solution.py:150
  668.9 4.8 convolution_convert_fusion.1
  676.3 4.1 fusion.15
  680.4 33.3 %all-gather.18.cloned.1.call-done = bf16[1024,1024]{1,0:T(8,128)(2,1)} async-done(((bf16[256,1024]{1,0:T(8,128)(2,1)}), bf16[1024,1024]{1,0:T(8,128)(2,1)}) %all-gather.18.cloned.1.call-update) | async-done | bytes 2097168 | tf_op jit(solution)/shard_map/all_gather | solution.py:146
  713.7 8.5 convert_reduce_fusion.1
  727.3 4.2 add_convert_fusion
  735.4 23.7 %collective-permute-done.32 = bf16[512,1024]{1,0:T(8,128)(2,1)} collective-permute-done((bf16[512,1024]{1,0:T(8,128)(2,1)}, bf16[512,1024]{1,0:T(8,128)(2,1)}, u32[]{:S(2)}, u32[]{:S(2)}) %collective-permute-start.32) | collective-permute-done | bytes 1048608 | tf_op jit(solution)/shard_map/ppermute | solution.py:168
  762.1 4.6 collective-permute-start.33
  766.7 4.0 convolution_convert_fusion.3
  773.4 4.1 fusion.17
  780.6 4.1 reshape.394
  795.0 4.2 add_convert_fusion.1
  804.5 4.6 collective-permute-start.10
  821.3 6.5 collective-permute-done.27
  830.8 29.8 %collective-permute-done.22 = bf16[256,1024]{1,0:T(8,128)(2,1)S(1)} collective-permute-done((bf16[256,1024]{1,0:T(8,128)(2,1)S(1)}, bf16[256,1024]{1,0:T(8,128)(2,1)S(1)}, u32[]{:S(2)}, u32[]{:S(2)}) %collective-permute-start.22) | collective-permute-done | bytes 524320 | tf_op jit(solution)/shard_map/ppermute | solution.py:168
  864.5 8.4 collective-permute-done.23
  880.9 13.7 %attend_backward.3 = (bf16[1024,256]{1,0:T(8,128)(2,1)S(1)}, bf16[1024,256]{1,0:T(8,128)(2,1)S(1)}, bf16[1024,256]{1,0:T(8,128)(2,1)S(1)}) custom-call(bf16[1024,768]{1,0:T(8,128)(2,1)S(1)} %add_convert_fusion.3.query_ref.key_ref.value_ref, bf16[1024,768]{1,0:T(8,128)(2,1)S(1)} %add_convert_fusion.3.query_ref.key_ref.value_ref, ...), custom_call_target="tpu_custom_call" | custom-call | flops 2684354560 | bytes 4718592 | tf_op jit(solution)/shard_map/attend_backward/pallas_call | solution.py:127
  922.1 5.1 broadcast_select_fusion.1
  935.3 5.4 collective-permute-start.15
  941.1 5.4 collective-permute-done.18
  948.4 11.3 %collective-permute-done.19 = bf16[256,1024]{1,0:T(8,128)(2,1)S(1)} collective-permute-done((bf16[256,1024]{1,0:T(8,128)(2,1)S(1)}, bf16[256,1024]{1,0:T(8,128)(2,1)S(1)}, u32[]{:S(2)}, u32[]{:S(2)}) %collective-permute-start.19) | collective-permute-done | bytes 524320 | tf_op jit(solution)/shard_map/ppermute | solution.py:168
  965.4 4.2 slice_bitcast_fusion
  985.1 5.8 reshape.395
  991.0 4.5 copy.29
  996.7 100.9 %all-reduce.2.cloned.1.call-done = f32[24576]{0:T(1024)} async-done(((f32[24576]{0:T(1024)}), f32[24576]{0:T(1024)}) %all-reduce.2.cloned.1.call-update) | async-done | bytes 98320 | tf_op jit(solution)/shard_map/psum | solution.py:367
  (468 shorter events, 230.5 us)
Async XLA Ops:
  7.2 61.2 %all-gather.8.cloned.1.call-start = ((), (), s32[]{:S(2)}) async-start(), calls=%async_computation.8 | async-start | bytes 2621440 | tf_op jit(solution)/shard_map/all_gather | solution.py:146
  21.9 122.0 %reduce-scatter.9.cloned.1.call-start = ((), (), s32[]{:S(2)}) async-start(), calls=%async_computation.9 | async-start | bytes 2621440 | tf_op jit(solution)/shard_map/reduce_scatter | solution.py:150
  23.9 20.6 %collective-permute-start.1 = (bf16[512,768]{0,1:T(8,128)(2,1)S(1)}, bf16[512,768]{0,1:T(8,128)(2,1)}, u32[]{:S(2)}, u32[]{:S(2)}) collective-permute-start(bf16[512,768]{0,1:T(8,128)(2,1)S(1)} %constant_dynamic-slice_fusion.5), channel_id=1, source_target_pairs={{0,16},{16,0},{1,17},{17,1},{2,18},{18,2},{3,19},{19,3},{4,20},{20... | collective-permute-start | bytes 2359304 | tf_op jit(solution)/shard_map/ppermute | solution.py:183
  24.7 23.9 %collective-permute-start.3 = (bf16[128,1024]{1,0:T(8,128)(2,1)S(1)}, bf16[128,1024]{1,0:T(8,128)(2,1)S(1)}, u32[]{:S(2)}, u32[]{:S(2)}) collective-permute-start(bf16[128,1024]{1,0:T(8,128)(2,1)S(1)} %dynamic-slice_bitcast_fusion.3), channel_id=1, source_target_pairs={{0,16},{16,0},{1,17},{17,1},{2,18},{18,2},{3,19},{19,3},{4,20},{20... | collective-permute-start | bytes 786440 | tf_op jit(solution)/shard_map/ppermute | solution.py:183
  85.3 107.4 %all-gather.10.cloned.1.call-start = ((), (), s32[]{:S(2)}) async-start(), calls=%async_computation.10 | async-start | bytes 2621440 | tf_op jit(solution)/shard_map/all_gather | solution.py:146
  87.1 26.1 %collective-permute-start.5 = (bf16[512,1024]{1,0:T(8,128)(2,1)S(1)}, bf16[512,1024]{1,0:T(8,128)(2,1)S(1)}, u32[]{:S(2)}, u32[]{:S(2)}) collective-permute-start(bf16[512,1024]{1,0:T(8,128)(2,1)S(1)} %dynamic-slice_bitcast_fusion.1), channel_id=1, source_target_pairs={{0,16},{16,0},{1,17},{17,1},{2,18},{18,2},{3,19},{19,3},{4,20},{20... | collective-permute-start | bytes 3145736 | tf_op jit(solution)/shard_map/ppermute | solution.py:183
  88.7 45.8 %collective-permute-start.7 = (bf16[512,1024]{1,0:T(8,128)(2,1)S(1)}, bf16[512,1024]{1,0:T(8,128)(2,1)S(1)}, u32[]{:S(2)}, u32[]{:S(2)}) collective-permute-start(bf16[512,1024]{1,0:T(8,128)(2,1)S(1)} %dynamic-slice_bitcast_fusion), channel_id=1, source_target_pairs={{0,16},{16,0},{1,17},{17,1},{2,18},{18,2},{3,19},{19,3},{4,20},{20... | collective-permute-start | bytes 3145736 | tf_op jit(solution)/shard_map/ppermute | solution.py:183
  113.2 21.3 %collective-permute-start.6 = (bf16[512,1024]{1,0:T(8,128)(2,1)S(1)}, bf16[512,1024]{1,0:T(8,128)(2,1)S(1)}, u32[]{:S(2)}, u32[]{:S(2)}) collective-permute-start(bf16[512,1024]{1,0:T(8,128)(2,1)S(1)} %collective-permute-done.5), channel_id=1, source_target_pairs={{0,1},{1,0},{2,3},{3,2},{4,5},{5,4},{6,7},{7,6},{8,9},{9,8},{10,11... | collective-permute-start | bytes 3145736 | tf_op jit(solution)/shard_map/ppermute | solution.py:168
  147.7 98.6 %reduce-scatter.11.cloned.1.call-start = ((), (), s32[]{:S(2)}) async-start(), calls=%async_computation.11 | async-start | bytes 2621440 | tf_op jit(solution)/shard_map/reduce_scatter | solution.py:150
  203.6 90.8 %all-gather.12.cloned.1.call-start = ((), (), s32[]{:S(2)}) async-start(), calls=%async_computation.12 | async-start | bytes 2621440 | tf_op jit(solution)/shard_map/all_gather | solution.py:146
  249.0 104.5 %reduce-scatter.13.cloned.1.call-start = ((), (), s32[]{:S(2)}) async-start(), calls=%async_computation.13 | async-start | bytes 2621440 | tf_op jit(solution)/shard_map/reduce_scatter | solution.py:150
  310.2 125.8 %all-gather.14.cloned.1.call-start = ((), (), s32[]{:S(2)}) async-start(), calls=%async_computation.14 | async-start | bytes 2621440 | tf_op jit(solution)/shard_map/all_gather | solution.py:146
  356.9 144.5 %reduce-scatter.17.cloned.1.call-start = ((), (), s32[]{:S(2)}) async-start(), calls=%async_computation.16 | async-start | bytes 2621440 | tf_op jit(solution)/shard_map/reduce_scatter | solution.py:150
  358.4 23.3 %collective-permute-start.11 = (bf16[256,1024]{1,0:T(8,128)(2,1)S(1)}, bf16[256,1024]{1,0:T(8,128)(2,1)}, u32[]{:S(2)}, u32[]{:S(2)}) collective-permute-start(bf16[256,1024]{1,0:T(8,128)(2,1)S(1)} %get-tuple-element.89), channel_id=1, source_target_pairs={{0,4},{4,8},{8,12},{12,0},{1,5},{5,9},{9,13},{13,1},{2,6},{6,10},{... | collective-permute-start | bytes 1572872 | tf_op jit(solution)/shard_map/ppermute | solution.py:161
  359.7 61.5 %collective-permute-start.12 = (bf16[256,1024]{1,0:T(8,128)(2,1)S(1)}, bf16[256,1024]{1,0:T(8,128)(2,1)}, u32[]{:S(2)}, u32[]{:S(2)}) collective-permute-start(bf16[256,1024]{1,0:T(8,128)(2,1)S(1)} %get-tuple-element.89), channel_id=1, source_target_pairs={{0,8},{4,12},{8,0},{12,4},{1,9},{5,13},{9,1},{13,5},{2,10},{6,14},... | collective-permute-start | bytes 1572872 | tf_op jit(solution)/shard_map/ppermute | solution.py:161
  361.4 61.6 %collective-permute-start.13 = (bf16[256,1024]{1,0:T(8,128)(2,1)S(1)}, bf16[256,1024]{1,0:T(8,128)(2,1)S(1)}, u32[]{:S(2)}, u32[]{:S(2)}) collective-permute-start(bf16[256,1024]{1,0:T(8,128)(2,1)S(1)} %get-tuple-element.89), channel_id=1, source_target_pairs={{0,12},{4,0},{8,4},{12,8},{1,13},{5,1},{9,5},{13,9},{2,14},{6,2},{... | collective-permute-start | bytes 1572872 | tf_op jit(solution)/shard_map/ppermute | solution.py:161
  450.9 96.1 %reduce-scatter.15.cloned.1.call-start = ((), (), s32[]{:S(2)}) async-start(), calls=%async_computation.15 | async-start | bytes 2621440 | tf_op jit(solution)/shard_map/reduce_scatter | solution.py:150
  458.0 138.9 %all-gather.16.cloned.1.call-start = ((), (), s32[]{:S(2)}) async-start(), calls=%async_computation.17 | async-start | bytes 2621440 | tf_op jit(solution)/shard_map/all_gather | solution.py:146
  551.4 110.8 %reduce-scatter.19.cloned.1.call-start = ((), (), s32[]{:S(2)}) async-start(), calls=%async_computation.18 | async-start | bytes 2621440 | tf_op jit(solution)/shard_map/reduce_scatter | solution.py:150
  619.5 94.2 %all-gather.18.cloned.1.call-start = ((), (), s32[]{:S(2)}) async-start(), calls=%async_computation.19 | async-start | bytes 2621440 | tf_op jit(solution)/shard_map/all_gather | solution.py:146
  668.3 121.3 %reduce-scatter.21.cloned.1.call-start = ((), (), s32[]{:S(2)}) async-start(), calls=%async_computation.20 | async-start | bytes 2621440 | tf_op jit(solution)/shard_map/reduce_scatter | solution.py:150
  680.4 46.9 %collective-permute-start.31 = (bf16[1024,1024]{1,0:T(8,128)(2,1)}, bf16[1024,1024]{1,0:T(8,128)(2,1)}, u32[]{:S(2)}, u32[]{:S(2)}) collective-permute-start(bf16[1024,1024]{1,0:T(8,128)(2,1)} %fusion.15), channel_id=1, source_target_pairs={{0,1},{1,0},{2,3},{3,2},{4,5},{5,4},{6,7},{7,6},{8,9},{9,8},{10,11... | collective-permute-start | bytes 6291464 | tf_op jit(solution)/shard_map/ppermute | solution.py:168
  727.3 150.1 %all-gather.20.cloned.1.call-start = ((), (), s32[]{:S(2)}) async-start(), calls=%async_computation.21 | async-start | bytes 2621440 | tf_op jit(solution)/shard_map/all_gather | solution.py:146
  733.9 25.2 %collective-permute-start.32 = (bf16[512,1024]{1,0:T(8,128)(2,1)}, bf16[512,1024]{1,0:T(8,128)(2,1)}, u32[]{:S(2)}, u32[]{:S(2)}) collective-permute-start(bf16[512,1024]{1,0:T(8,128)(2,1)} %constant_dynamic-slice_fusion), channel_id=1, source_target_pairs={{0,2},{1,3},{2,0},{3,1},{4,6},{5,7},{6,4},{7,5},{8,10},{9,11},{10,... | collective-permute-start | bytes 3145736 | tf_op jit(solution)/shard_map/ppermute | solution.py:168
  762.1 47.0 %collective-permute-start.33 = (bf16[512,1024]{1,0:T(8,128)(2,1)}, bf16[512,1024]{1,0:T(8,128)(2,1)}, u32[]{:S(2)}, u32[]{:S(2)}) collective-permute-start(bf16[512,1024]{1,0:T(8,128)(2,1)} %add_convert_fusion.5), channel_id=1, source_target_pairs={{0,16},{1,17},{2,18},{3,19},{4,20},{5,21},{6,22},{7,23},{8,24},{9,... | collective-permute-start | bytes 3145736 | tf_op jit(solution)/shard_map/ppermute | solution.py:203
  777.5 17.5 %collective-permute-start.26 = (bf16[1024,1024]{1,0:T(8,128)(2,1)}, bf16[1024,1024]{1,0:T(8,128)(2,1)}, u32[]{:S(2)}, u32[]{:S(2)}) collective-permute-start(bf16[1024,1024]{1,0:T(8,128)(2,1)} %fusion.17), channel_id=1, source_target_pairs={{0,1},{1,0},{2,3},{3,2},{4,5},{5,4},{6,7},{7,6},{8,9},{9,8},{10,11... | collective-permute-start | bytes 6291464 | tf_op jit(solution)/shard_map/ppermute | solution.py:168
  789.1 22.5 %collective-permute-start.21 = (bf16[512,1024]{1,0:T(8,128)(2,1)}, bf16[512,1024]{1,0:T(8,128)(2,1)}, u32[]{:S(2)}, u32[]{:S(2)}) collective-permute-start(bf16[512,1024]{1,0:T(8,128)(2,1)} %fusion.54), channel_id=1, source_target_pairs={{0,1},{1,0},{2,3},{3,2},{4,5},{5,4},{6,7},{7,6},{8,9},{9,8},{10,11... | collective-permute-start | bytes 3145736 | tf_op jit(solution)/shard_map/ppermute | solution.py:168
  795.0 179.2 %reduce-scatter.23.cloned.1.call-start = ((), (), s32[]{:S(2)}) async-start(), calls=%async_computation.22 | async-start | bytes 2621440 | tf_op jit(solution)/shard_map/reduce_scatter | solution.py:150
  801.6 26.3 %collective-permute-start.27 = (bf16[512,1024]{1,0:T(8,128)(2,1)}, bf16[512,1024]{1,0:T(8,128)(2,1)}, u32[]{:S(2)}, u32[]{:S(2)}) collective-permute-start(bf16[512,1024]{1,0:T(8,128)(2,1)} %constant_dynamic-slice_fusion.1), channel_id=1, source_target_pairs={{0,2},{1,3},{2,0},{3,1},{4,6},{5,7},{6,4},{7,5},{8,10},{9,11},{10,... | collective-permute-start | bytes 3145736 | tf_op jit(solution)/shard_map/ppermute | solution.py:168
  803.0 15.6 %collective-permute-start.9 = (bf16[256,1024]{1,0:T(8,128)(2,1)S(1)}, bf16[256,1024]{1,0:T(8,128)(2,1)S(1)}, u32[]{:S(2)}, u32[]{:S(2)}) collective-permute-start(bf16[256,1024]{1,0:T(8,128)(2,1)S(1)} %copy-done.12), channel_id=1, source_target_pairs={{16,0},{17,1},{18,2},{19,3},{20,4},{21,5},{22,6},{23,7},{24,8},{25... | collective-permute-start | bytes 1572872 | tf_op jit(solution)/shard_map/ppermute | solution.py:351
  804.5 15.7 %collective-permute-start.10 = (bf16[256,1024]{1,0:T(8,128)(2,1)}, bf16[256,1024]{1,0:T(8,128)(2,1)S(1)}, u32[]{:S(2)}, u32[]{:S(2)}) collective-permute-start(bf16[256,1024]{1,0:T(8,128)(2,1)} %get-tuple-element.126), channel_id=1, source_target_pairs={{0,16},{1,17},{2,18},{3,19},{4,20},{5,21},{6,22},{7,23},{8,24},{9,... | collective-permute-start | bytes 1572872 | tf_op jit(solution)/shard_map/ppermute | solution.py:352
  811.1 51.1 %collective-permute-start.34 = (bf16[512,1024]{1,0:T(8,128)(2,1)S(1)}, bf16[512,1024]{1,0:T(8,128)(2,1)S(1)}, u32[]{:S(2)}, u32[]{:S(2)}) collective-permute-start(bf16[512,1024]{1,0:T(8,128)(2,1)S(1)} %add_convert_fusion.4), channel_id=1, source_target_pairs={{0,2},{1,3},{2,0},{3,1},{4,6},{5,7},{6,4},{7,5},{8,10},{9,11},{10,... | collective-permute-start | bytes 3145736 | tf_op jit(solution)/shard_map/ppermute | solution.py:168
  814.1 46.5 %collective-permute-start.22 = (bf16[256,1024]{1,0:T(8,128)(2,1)S(1)}, bf16[256,1024]{1,0:T(8,128)(2,1)S(1)}, u32[]{:S(2)}, u32[]{:S(2)}) collective-permute-start(bf16[256,1024]{1,0:T(8,128)(2,1)S(1)} %constant_dynamic-slice_fusion.2), channel_id=1, source_target_pairs={{0,2},{1,3},{2,0},{3,1},{4,6},{5,7},{6,4},{7,5},{8,10},{9,11},{10,... | collective-permute-start | bytes 1572872 | tf_op jit(solution)/shard_map/ppermute | solution.py:168
  829.5 45.9 %collective-permute-start.28 = (bf16[512,1024]{1,0:T(8,128)(2,1)S(1)}, bf16[512,1024]{1,0:T(8,128)(2,1)S(1)}, u32[]{:S(2)}, u32[]{:S(2)}) collective-permute-start(bf16[512,1024]{1,0:T(8,128)(2,1)S(1)} %add_convert_fusion.7), channel_id=1, source_target_pairs={{16,0},{17,1},{18,2},{19,3},{20,4},{21,5},{22,6},{23,7},{24,8},{25... | collective-permute-start | bytes 3145736 | tf_op jit(solution)/shard_map/ppermute | solution.py:203
  860.8 12.1 %collective-permute-start.23 = (bf16[256,1024]{1,0:T(8,128)(2,1)S(1)}, bf16[256,1024]{1,0:T(8,128)(2,1)S(1)}, u32[]{:S(2)}, u32[]{:S(2)}) collective-permute-start(bf16[256,1024]{1,0:T(8,128)(2,1)S(1)} %add_convert_fusion.11), channel_id=1, source_target_pairs={{0,16},{1,17},{2,18},{3,19},{4,20},{5,21},{6,22},{7,23},{8,24},{9,... | collective-permute-start | bytes 1572872 | tf_op jit(solution)/shard_map/ppermute | solution.py:203
  864.3 56.4 %collective-permute-start.35 = (bf16[1024,1024]{1,0:T(8,128)(2,1)}, bf16[1024,1024]{1,0:T(8,128)(2,1)}, u32[]{:S(2)}, u32[]{:S(2)}) collective-permute-start(bf16[1024,1024]{1,0:T(8,128)(2,1)} %pad_maximum_fusion.3), channel_id=1, source_target_pairs={{0,1},{1,0},{2,3},{3,2},{4,5},{5,4},{6,7},{7,6},{8,9},{9,8},{10,11... | collective-permute-start | bytes 6291464 | tf_op jit(solution)/shard_map/ppermute | solution.py:168
  873.9 32.0 %collective-permute-start.24 = (bf16[256,1024]{1,0:T(8,128)(2,1)}, bf16[256,1024]{1,0:T(8,128)(2,1)}, u32[]{:S(2)}, u32[]{:S(2)}) collective-permute-start(bf16[256,1024]{1,0:T(8,128)(2,1)} %add_convert_fusion.10), channel_id=1, source_target_pairs={{0,2},{1,3},{2,0},{3,1},{4,6},{5,7},{6,4},{7,5},{8,10},{9,11},{10,... | collective-permute-start | bytes 1572872 | tf_op jit(solution)/shard_map/ppermute | solution.py:168
  876.8 32.3 %collective-permute-start.29 = (bf16[512,1024]{1,0:T(8,128)(2,1)}, bf16[512,1024]{1,0:T(8,128)(2,1)}, u32[]{:S(2)}, u32[]{:S(2)}) collective-permute-start(bf16[512,1024]{1,0:T(8,128)(2,1)} %add_convert_fusion.6), channel_id=1, source_target_pairs={{0,2},{1,3},{2,0},{3,1},{4,6},{5,7},{6,4},{7,5},{8,10},{9,11},{10,... | collective-permute-start | bytes 3145736 | tf_op jit(solution)/shard_map/ppermute | solution.py:168
  905.7 7.3 collective-permute-start.16
  908.4 23.7 %collective-permute-start.25 = (bf16[512,1024]{1,0:T(8,128)(2,1)}, bf16[512,1024]{1,0:T(8,128)(2,1)}, u32[]{:S(2)}, u32[]{:S(2)}) collective-permute-start(bf16[512,1024]{1,0:T(8,128)(2,1)} %pad_maximum_fusion.6), channel_id=1, source_target_pairs={{0,1},{1,0},{2,3},{3,2},{4,5},{5,4},{6,7},{7,6},{8,9},{9,8},{10,11... | collective-permute-start | bytes 3145736 | tf_op jit(solution)/shard_map/ppermute | solution.py:168
  912.9 47.0 %collective-permute-start.30 = (bf16[1024,1024]{1,0:T(8,128)(2,1)}, bf16[1024,1024]{1,0:T(8,128)(2,1)}, u32[]{:S(2)}, u32[]{:S(2)}) collective-permute-start(bf16[1024,1024]{1,0:T(8,128)(2,1)} %pad_maximum_fusion.2), channel_id=1, source_target_pairs={{0,1},{1,0},{2,3},{3,2},{4,5},{5,4},{6,7},{7,6},{8,9},{9,8},{10,11... | collective-permute-start | bytes 6291464 | tf_op jit(solution)/shard_map/ppermute | solution.py:168
  916.0 14.5 %collective-permute-start.17 = (bf16[256,1024]{1,0:T(8,128)(2,1)}, bf16[256,1024]{1,0:T(8,128)(2,1)S(1)}, u32[]{:S(2)}, u32[]{:S(2)}) collective-permute-start(bf16[256,1024]{1,0:T(8,128)(2,1)} %constant_dynamic-slice_fusion.4), channel_id=1, source_target_pairs={{0,2},{1,3},{2,0},{3,1},{4,6},{5,7},{6,4},{7,5},{8,10},{9,11},{10,... | collective-permute-start | bytes 1572872 | tf_op jit(solution)/shard_map/ppermute | solution.py:168
  920.6 177.0 %all-reduce.2.cloned.1.call-start = ((), (), s32[]{:S(2)}) async-start(), calls=%async_computation.23 | async-start | bytes 196608 | tf_op jit(solution)/shard_map/psum | solution.py:367
  930.7 15.8 %collective-permute-start.18 = (bf16[256,1024]{1,0:T(8,128)(2,1)S(1)}, bf16[256,1024]{1,0:T(8,128)(2,1)S(1)}, u32[]{:S(2)}, u32[]{:S(2)}) collective-permute-start(bf16[256,1024]{1,0:T(8,128)(2,1)S(1)} %add_convert_fusion.13), channel_id=1, source_target_pairs={{16,0},{17,1},{18,2},{19,3},{20,4},{21,5},{22,6},{23,7},{24,8},{25... | collective-permute-start | bytes 1572872 | tf_op jit(solution)/shard_map/ppermute | solution.py:203
  935.3 165.8 %collective-permute-start.15 = (bf16[256,1024]{1,0:T(8,128)(2,1)S(1)}, bf16[256,1024]{1,0:T(8,128)(2,1)}, u32[]{:S(2)}, u32[]{:S(2)}) collective-permute-start(bf16[256,1024]{1,0:T(8,128)(2,1)S(1)} %copy-done.18), channel_id=1, source_target_pairs={{0,16},{1,17},{2,18},{3,19},{4,20},{5,21},{6,22},{7,23},{8,24},{9,... | collective-permute-start | bytes 1572872 | tf_op jit(solution)/shard_map/ppermute | solution.py:352
  946.7 13.1 %collective-permute-start.19 = (bf16[256,1024]{1,0:T(8,128)(2,1)S(1)}, bf16[256,1024]{1,0:T(8,128)(2,1)S(1)}, u32[]{:S(2)}, u32[]{:S(2)}) collective-permute-start(bf16[256,1024]{1,0:T(8,128)(2,1)S(1)} %add_convert_fusion.12), channel_id=1, source_target_pairs={{0,2},{1,3},{2,0},{3,1},{4,6},{5,7},{6,4},{7,5},{8,10},{9,11},{10,... | collective-permute-start | bytes 1572872 | tf_op jit(solution)/shard_map/ppermute | solution.py:168
  959.9 9.7 collective-permute-start.20
  995.4 105.7 %collective-permute-start.14 = (bf16[256,1024]{1,0:T(8,128)(2,1)S(1)}, bf16[256,1024]{1,0:T(8,128)(2,1)S(1)}, u32[]{:S(2)}, u32[]{:S(2)}) collective-permute-start(bf16[256,1024]{1,0:T(8,128)(2,1)S(1)} %get-tuple-element.118), channel_id=1, source_target_pairs={{16,0},{17,1},{18,2},{19,3},{20,4},{21,5},{22,6},{23,7},{24,8},{25... | collective-permute-start | bytes 1572872 | tf_op jit(solution)/shard_map/ppermute | solution.py:351
  (110 other events, 985.3 us)
Sparse Core Ops, SparseCore 0:
  22.0 46.3 all-gather.7
  85.4 42.5 reduce-scatter.8
  147.8 44.8 all-gather.9
  203.7 42.5 reduce-scatter.10
  249.1 45.2 all-gather.11
  310.4 43.0 reduce-scatter.12
  357.0 78.9 all-gather.13
  451.0 50.4 reduce-scatter.16
  503.7 43.1 reduce-scatter.14
  551.6 45.2 all-gather.15
  619.6 42.5 reduce-scatter.18
  668.5 45.2 all-gather.17
  727.4 42.5 reduce-scatter.20
  795.1 43.9 all-gather.19
  920.7 42.9 reduce-scatter.22
  979.0 118.5 all-reduce.1
